TPU v7x, 128 devices: a whole 4x4x4 slice. The times are simulated.
128 devices in a mesh: rows: 8 (over x, core), cols: 16 (over y, z).
Axes of the slice: x: 4, y: 4, z: 4, core: 2. Of those that a mesh axis runs over, the one named last changes fastest.
Arguments:
- momentum: float32 [8192, 26624], P('rows', 'cols'), may hold values from -40 to 40
- grad: bfloat16 [8192, 26624], P('rows', 'cols'), may hold values from -20 to 20
- q_basis: bfloat16 [26624, 512], P('cols'), may hold values from -6 to 6
Outputs:
- mom_next: float32 [8192, 26624], P('rows', 'cols')
- q_next: bfloat16 [26624, 512], P('cols')
- update: bfloat16 [8192, 26624], P('rows', 'cols')
All inputs are finite; a program needn't handle non-finite values.
Results may differ from a plain program's by a relative error of at most 0.0029.
Values sent between devices are 32-bit elements; how exact they have to be, the bound alone decides.
A program may use at most 128 MiB of HBM per device.

v0:
```python
import jax
import jax.numpy as jnp
from jax import lax
from jax.sharding import PartitionSpec as P

ROWS = 8192
COLS = 26624
RANK = 512


feedback_rate = 0.05
epsilon = 1e-05


def partner_2(x, axis, apart):
    return lax.ppermute(x, axis, [(i, i ^ 1 << apart) for i in range(lax.axis_size(axis))])


def exact_dot(left, right_side):
    return jnp.dot(
        left, right_side, precision=lax.Precision.HIGHEST, preferred_element_type=jnp.float32
    )


def dot_over_rows(left, right_side):
    return lax.dot_general(
        left,
        right_side,
        (((0,), (0,)), ((), ())),
        precision=lax.Precision.HIGHEST,
        preferred_element_type=jnp.float32,
    )


def apply_factor(low_factor, matrix):
    return jax.scipy.linalg.solve_triangular(low_factor, matrix.T, lower=True).T


def body(momentum, grad, q_basis):
    merged = momentum + grad.astype(jnp.float32)
    q_float_in = q_basis.astype(jnp.float32)
    projected = lax.psum(exact_dot(merged, q_float_in), "cols")
    gram_local = dot_over_rows(projected, projected)
    low_factor = jnp.linalg.cholesky(gram_local)
    for level in range(lax.axis_size("rows").bit_length() - 1):
        partner = partner_2(low_factor, "rows", level)
        low_factor = jnp.linalg.cholesky(
            exact_dot(low_factor, low_factor.T) + exact_dot(partner, partner.T)
        )
    orth_basis = apply_factor(low_factor, projected)
    right_factor = lax.psum(dot_over_rows(merged, orth_basis), "rows")
    column_sum = lax.psum(jnp.sum(right_factor * right_factor, axis=0), "cols")
    mom_next = merged - feedback_rate * exact_dot(orth_basis, right_factor.T)
    column_sq = column_sum / COLS
    q_float = right_factor * lax.rsqrt(column_sq + epsilon)
    update = (jnp.sqrt(jnp.float32(ROWS) / RANK) * exact_dot(orth_basis, q_float.T)).astype(
        jnp.bfloat16
    )
    return (mom_next, q_float.astype(jnp.bfloat16), update)


def solution(mesh):
    return jax.shard_map(
        body,
        mesh=mesh,
        in_specs=(P("rows", "cols"), P("rows", "cols"), P("cols", None)),
        out_specs=(P("rows", "cols"), P("cols", None), P("rows", "cols")),
        check_vma=False,
    )
```

profile of v0, /device:TPU:0, one launch (start us, length us, event | category | flops | bytes accessed | tf_op | source)
XLA Modules:
  0.0 796.7 jit_solution(726676574043199906)
XLA Ops:
  18.4 92.8 %all-reduce.4.cloned.1.call-done = f32[1024,512]{1,0:T(8,128)} async-done(((f32[1024,512]{1,0:T(8,128)}), f32[1024,512]{1,0:T(8,128)}) %all-reduce.4.cloned.1.call-update) | async-done | bytes 2097168 | tf_op jit(solution)/shard_map/psum | solution.py:42
  118.4 11.7 %cholesky.462 = f32[128,128]{1,0:T(8,128)S(1)} custom-call(f32[128,128]{1,0:T(8,128)S(1)} %cholesky.746), custom_call_target="Cholesky" | custom-call | tf_op jit(solution)/shard_map/jit(cholesky)/cholesky | solution.py:44
  130.2 9.8 %custom-call.34 = f32[1,128,128]{1,2,0:T(8,128)S(1)} custom-call(f32[1,128,128]{2,1,0:T(8,128)S(1)} %get-tuple-element.61), custom_call_target="InvertDiagBlocksLowerTriangular" | custom-call | tf_op jit(solution)/shard_map/jit(cholesky)/cholesky | solution.py:44
  142.7 12.1 %cholesky.481 = f32[128,128]{1,0:T(8,128)S(1)} custom-call(f32[128,128]{1,0:T(8,128)S(1)} %cholesky.750), custom_call_target="Cholesky" | custom-call | tf_op jit(solution)/shard_map/jit(cholesky)/cholesky | solution.py:44
  154.8 9.8 %custom-call.35 = f32[1,128,128]{1,2,0:T(8,128)S(1)} custom-call(f32[1,128,128]{2,1,0:T(8,128)S(1)} %get-tuple-element.58), custom_call_target="InvertDiagBlocksLowerTriangular" | custom-call | tf_op jit(solution)/shard_map/jit(cholesky)/cholesky | solution.py:44
  166.2 11.7 %cholesky.502 = f32[128,128]{1,0:T(8,128)S(1)} custom-call(f32[128,128]{1,0:T(8,128)S(1)} %cholesky.755), custom_call_target="Cholesky" | custom-call | tf_op jit(solution)/shard_map/jit(cholesky)/cholesky | solution.py:44
  178.6 9.8 %custom-call.36 = f32[1,128,128]{1,2,0:T(8,128)S(1)} custom-call(f32[1,128,128]{2,1,0:T(8,128)S(1)} %get-tuple-element.55), custom_call_target="InvertDiagBlocksLowerTriangular" | custom-call | tf_op jit(solution)/shard_map/jit(cholesky)/cholesky | solution.py:44
  189.8 11.9 %cholesky.519 = f32[128,128]{1,0:T(8,128)S(1)} custom-call(f32[128,128]{1,0:T(8,128)S(1)} %convolution_subtract_fusion.4), custom_call_target="Cholesky" | custom-call | tf_op jit(solution)/shard_map/jit(cholesky)/cholesky | solution.py:44
  211.9 11.7 %cholesky.534 = f32[128,128]{1,0:T(8,128)S(1)} custom-call(f32[128,128]{1,0:T(8,128)S(1)} %cholesky.759), custom_call_target="Cholesky" | custom-call | tf_op jit(solution)/shard_map/jit(cholesky)/cholesky | solution.py:47
  224.4 9.8 %custom-call.37 = f32[1,128,128]{1,2,0:T(8,128)S(1)} custom-call(f32[1,128,128]{2,1,0:T(8,128)S(1)} %get-tuple-element.51), custom_call_target="InvertDiagBlocksLowerTriangular" | custom-call | tf_op jit(solution)/shard_map/jit(cholesky)/cholesky | solution.py:47
  236.7 12.1 %cholesky.553 = f32[128,128]{1,0:T(8,128)S(1)} custom-call(f32[128,128]{1,0:T(8,128)S(1)} %cholesky.763), custom_call_target="Cholesky" | custom-call | tf_op jit(solution)/shard_map/jit(cholesky)/cholesky | solution.py:47
  260.9 11.7 %cholesky.574 = f32[128,128]{1,0:T(8,128)S(1)} custom-call(f32[128,128]{1,0:T(8,128)S(1)} %cholesky.768), custom_call_target="Cholesky" | custom-call | tf_op jit(solution)/shard_map/jit(cholesky)/cholesky | solution.py:47
  284.7 11.7 %cholesky.591 = f32[128,128]{1,0:T(8,128)S(1)} custom-call(f32[128,128]{1,0:T(8,128)S(1)} %slice_subtract_fusion.8), custom_call_target="Cholesky" | custom-call | tf_op jit(solution)/shard_map/jit(cholesky)/cholesky | solution.py:47
  303.2 21.9 %collective-permute-done.1 = f32[512,512]{1,0:T(8,128)S(1)} collective-permute-done((f32[512,512]{1,0:T(8,128)S(1)}, f32[512,512]{1,0:T(8,128)S(1)}, u32[]{:S(2)}, u32[]{:S(2)}) %collective-permute-start.1) | collective-permute-done | bytes 1048608 | tf_op jit(solution)/shard_map/ppermute | solution.py:16
  328.5 11.7 %cholesky.606 = f32[128,128]{1,0:T(8,128)S(1)} custom-call(f32[128,128]{1,0:T(8,128)S(1)} %cholesky.772), custom_call_target="Cholesky" | custom-call | tf_op jit(solution)/shard_map/jit(cholesky)/cholesky | solution.py:47
  353.4 12.1 %cholesky.625 = f32[128,128]{1,0:T(8,128)S(1)} custom-call(f32[128,128]{1,0:T(8,128)S(1)} %cholesky.776), custom_call_target="Cholesky" | custom-call | tf_op jit(solution)/shard_map/jit(cholesky)/cholesky | solution.py:47
  366.1 9.8 %custom-call.41 = f32[1,128,128]{1,2,0:T(8,128)S(1)} custom-call(f32[1,128,128]{2,1,0:T(8,128)S(1)} %get-tuple-element.38), custom_call_target="InvertDiagBlocksLowerTriangular" | custom-call | tf_op jit(solution)/shard_map/jit(cholesky)/cholesky | solution.py:47
  377.5 11.7 %cholesky.646 = f32[128,128]{1,0:T(8,128)S(1)} custom-call(f32[128,128]{1,0:T(8,128)S(1)} %cholesky.781), custom_call_target="Cholesky" | custom-call | tf_op jit(solution)/shard_map/jit(cholesky)/cholesky | solution.py:47
  389.9 9.8 %custom-call.42 = f32[1,128,128]{1,2,0:T(8,128)S(1)} custom-call(f32[1,128,128]{2,1,0:T(8,128)S(1)} %get-tuple-element.35), custom_call_target="InvertDiagBlocksLowerTriangular" | custom-call | tf_op jit(solution)/shard_map/jit(cholesky)/cholesky | solution.py:47
  401.3 11.7 %cholesky.663 = f32[128,128]{1,0:T(8,128)S(1)} custom-call(f32[128,128]{1,0:T(8,128)S(1)} %slice_subtract_fusion.7), custom_call_target="Cholesky" | custom-call | tf_op jit(solution)/shard_map/jit(cholesky)/cholesky | solution.py:47
  421.3 21.0 %collective-permute-done.2 = f32[512,512]{1,0:T(8,128)S(1)} collective-permute-done((f32[512,512]{1,0:T(8,128)S(1)}, f32[512,512]{1,0:T(8,128)S(1)}, u32[]{:S(2)}, u32[]{:S(2)}) %collective-permute-start.2) | collective-permute-done | bytes 1048608 | tf_op jit(solution)/shard_map/ppermute | solution.py:16
  445.8 11.7 %cholesky.678 = f32[128,128]{1,0:T(8,128)S(1)} custom-call(f32[128,128]{1,0:T(8,128)S(1)} %cholesky.785), custom_call_target="Cholesky" | custom-call | tf_op jit(solution)/shard_map/jit(cholesky)/cholesky | solution.py:47
  458.3 9.8 %custom-call.43 = f32[1,128,128]{1,2,0:T(8,128)S(1)} custom-call(f32[1,128,128]{2,1,0:T(8,128)S(1)} %get-tuple-element.31), custom_call_target="InvertDiagBlocksLowerTriangular" | custom-call | tf_op jit(solution)/shard_map/jit(cholesky)/cholesky | solution.py:47
  470.6 12.1 %cholesky.697 = f32[128,128]{1,0:T(8,128)S(1)} custom-call(f32[128,128]{1,0:T(8,128)S(1)} %cholesky.789), custom_call_target="Cholesky" | custom-call | tf_op jit(solution)/shard_map/jit(cholesky)/cholesky | solution.py:47
  494.8 11.7 %cholesky.718 = f32[128,128]{1,0:T(8,128)S(1)} custom-call(f32[128,128]{1,0:T(8,128)S(1)} %cholesky.794), custom_call_target="Cholesky" | custom-call | tf_op jit(solution)/shard_map/jit(cholesky)/cholesky | solution.py:47
  518.7 11.7 %cholesky.735 = f32[128,128]{1,0:T(8,128)S(1)} custom-call(f32[128,128]{1,0:T(8,128)S(1)} %slice_subtract_fusion.6), custom_call_target="Cholesky" | custom-call | tf_op jit(solution)/shard_map/jit(cholesky)/cholesky | solution.py:47
  541.7 39.3 %custom-call.24 = f32[4,128,128]{1,2,0:T(8,128)S(1)} custom-call(f32[4,128,128]{2,1,0:T(8,128)S(1)} %get-tuple-element.11), custom_call_target="InvertDiagBlocksLowerTriangular" | custom-call | tf_op jit(solution)/shard_map/jit(_solve_triangular)/triangular_solve | solution.py:36
  593.7 27.2 %fusion.1 = f32[1664,512]{1,0:T(8,128)} fusion(f32[1024,1664]{1,0:T(8,128)} %param.4, bf16[1024,1664]{1,0:T(8,128)(2,1)S(1)} %copy-done.3, f32[128,1024]{1,0:T(8,128)S(1)} %fusion.54, f32[128,1024]{1,0:T(8,128)S(1)} %fusion.55, f32[128,1024]{1,0:T(8,128)S(1)} %fusion.57, f32[128,1024]{1,0:T(8,128)S(1)} %fusion.20), kind=kOutput, calls=%fused_computation.8 | convolution fusion | flops 10473963520 | bytes 15728640 | tf_op jit(solution)/shard_map/dot_general | solution.py:26
  621.0 69.4 %all-reduce.6.cloned.1.call-done = f32[1664,512]{1,0:T(8,128)} async-done(((f32[1664,512]{1,0:T(8,128)}), f32[1664,512]{1,0:T(8,128)}) %all-reduce.6.cloned.1.call-update) | async-done | bytes 3407888 | tf_op jit(solution)/shard_map/psum | solution.py:51
  692.6 40.6 %psum.23 = f32[512]{0:T(512)S(1)} all-reduce(f32[512]{0:T(512)S(1)} %multiply_reduce_fusion), channel_id=1, replica_groups=mesh['rows'=8,'cols'=16] {'cols'}, use_global_device_ids=true, to_apply=%region_11.13 | all-reduce | flops 512 | bytes 4096 | tf_op jit(solution)/shard_map/psum | solution.py:52
  737.0 26.6 %multiply_convert_fusion = bf16[1024,1664]{1,0:T(8,128)(2,1)} fusion(f32[1664,512]{1,0:T(8,128)} %all-reduce.6.cloned.1.call-done, f32[512]{0:T(512)S(1)} %add_rsqrt_fusion, f32[128,1024]{1,0:T(8,128)S(1)} %fusion.54, f32[128,1024]{1,0:T(8,128)S(1)} %fusion.55, f32[128,1024]{1,0:T(8,128)S(1)} %fusion.57, f32[128,1024]{1,0:T(8,128)S(1)} %fusion.20), kind=kOutput, calls=%fused_computation.2 | convolution fusion | flops 10474815488 | bytes 8914944 | tf_op jit(solution)/shard_map/dot_general | solution.py:20
  763.6 26.0 %multiply_subtract_fusion = f32[1024,1664]{1,0:T(8,128)} fusion(f32[1664,512]{1,0:T(8,128)S(1)} %copy-done.2, f32[1024,1664]{1,0:T(8,128)S(1)} %bitcast.132, bf16[1024,1664]{1,0:T(8,128)(2,1)S(1)} %copy-done.4, f32[128,1024]{1,0:T(8,128)} %copy-done.5, f32[128,1024]{1,0:T(8,128)S(1)} %fusion.55, f32[128,1024]{1,0:T(8,128)S(1)} %fusion.57, ...), kind=kOutput, calls=%fused_computation.3 | convolution fusion | flops 10477371392 | bytes 22544384 | tf_op jit(solution)/shard_map/dot_general | solution.py:20
  (157 shorter events, 156.6 us)
Async XLA Ops:
  7.2 1.5 copy-start
  7.2 104.0 %all-reduce.4.cloned.1.call-start = ((), (), s32[]{:S(2)}) async-start(), calls=%async_computation | async-start | bytes 4194304 | tf_op jit(solution)/shard_map/psum | solution.py:42
  18.1 672.2 %all-reduce.6.cloned.1.call-start = ((), (), s32[]{:S(2)}) async-start(), calls=%async_computation.1 | async-start | bytes 6815744 | tf_op jit(solution)/shard_map/psum | solution.py:51
  117.4 1.0 copy-start.10
  205.7 2.7 collective-permute-start
  210.9 1.0 copy-start.8
  299.8 25.3 %collective-permute-start.1 = (f32[512,512]{1,0:T(8,128)S(1)}, f32[512,512]{1,0:T(8,128)S(1)}, u32[]{:S(2)}, u32[]{:S(2)}) collective-permute-start(f32[512,512]{1,0:T(8,128)S(1)} %select_select_fusion.2), channel_id=1, source_target_pairs={{0,32},{16,48},{32,0},{48,16},{64,96},{80,112},{96,64},{112,80},{1... | collective-permute-start | bytes 3145736 | tf_op jit(solution)/shard_map/ppermute | solution.py:16
  327.5 1.0 copy-start.9
  416.4 25.9 %collective-permute-start.2 = (f32[512,512]{1,0:T(8,128)S(1)}, f32[512,512]{1,0:T(8,128)S(1)}, u32[]{:S(2)}, u32[]{:S(2)}) collective-permute-start(f32[512,512]{1,0:T(8,128)S(1)} %select_select_fusion.1), channel_id=1, source_target_pairs={{0,64},{16,80},{32,96},{48,112},{64,0},{80,16},{96,32},{112,48},{1... | collective-permute-start | bytes 3145736 | tf_op jit(solution)/shard_map/ppermute | solution.py:16
  444.8 1.0 copy-start.7
  541.7 41.0 %copy-start.6 = (f32[512,512]{1,0:T(8,128)}, f32[512,512]{1,0:T(8,128)S(1)}, u32[]{:S(2)}) copy-start(f32[512,512]{1,0:T(8,128)S(1)} %get-tuple-element.128) | copy-start | bytes 3145732
  589.0 4.6 copy-start.3
  593.7 143.3 %copy-start.5 = (f32[128,1024]{1,0:T(8,128)}, f32[128,1024]{1,0:T(8,128)S(1)}, u32[]{:S(2)}) copy-start(f32[128,1024]{1,0:T(8,128)S(1)} %fusion.54) | copy-start | bytes 1572868
  733.1 30.4 %slice-start = ((s8[6815744]{0:T(1024)(128)(4,1)}), s8[4194304]{0:T(1024)(128)(4,1)S(1)}, s32[]{:S(2)}) async-start(s8[6815744]{0:T(1024)(128)(4,1)} %bitcast.131), calls=%async_computation.2 | async-start | bytes 8388608
  736.9 26.7 %slice-start.1 = ((s8[6815744]{0:T(1024)(128)(4,1)}), s8[2621440]{0:T(1024)(128)(4,1)S(1)}, s32[]{:S(2)}) async-start(s8[6815744]{0:T(1024)(128)(4,1)} %bitcast.131), calls=%async_computation.3 | async-start | bytes 5242880
  736.9 26.7 %copy-start.2 = (f32[1664,512]{1,0:T(8,128)S(1)}, f32[1664,512]{1,0:T(8,128)}, u32[]{:S(2)}) copy-start(f32[1664,512]{1,0:T(8,128)} %all-reduce.6.cloned.1.call-done) | copy-start | bytes 10223620
  736.9 26.7 %copy-start.4 = (bf16[1024,1664]{1,0:T(8,128)(2,1)S(1)}, bf16[1024,1664]{1,0:T(8,128)(2,1)}, u32[]{:S(2)}) copy-start(bf16[1024,1664]{1,0:T(8,128)(2,1)} %param.5) | copy-start | bytes 10223620
  763.6 26.0 %copy-start.1 = (bf16[1664,512]{1,0:T(8,128)(2,1)S(1)}, bf16[1664,512]{1,0:T(8,128)(2,1)}, u32[]{:S(2)}) copy-start(bf16[1664,512]{1,0:T(8,128)(2,1)} %param.6) | copy-start | bytes 5111812
Sparse Core Ops, SparseCore 0:
  18.3 92.8 all-reduce.3
  621.1 69.1 all-reduce.5
where the time goes:
time: 800 us; the launch traced here: 797 us
  other arithmetic  364 us (46%)
  waiting for transfers between devices  206 us (26%)
  matrix products  141 us (18%)
  blocking collectives  40.6 us (5%)
  between operations  25.6 us (3%)
  local copies, waits for them, and re-layouts  15.1 us (2%)
    another operation x45, other arithmetic, body(): jnp.linalg.cholesky(exact_dot(low_factor, low_factor.T) + exact_dot(partn...  238 us
    psum x1, waiting for transfers between devices, body(): projected = lax.psum(exact_dot(merged, q_float_in), 'cols')  92.8 us
    another operation x14, other arithmetic, body(): low_factor = jnp.linalg.cholesky(gram_local)  78.9 us
    dot_general x9, matrix products, exact_dot(): jnp.dot(left, right_side, precision=lax.Precision.HIGHEST, preferred_elem...  73.3 us
    psum x1, waiting for transfers between devices, body(): right_factor = lax.psum(dot_over_rows(merged, orth_basis), 'rows')  69.4 us
    ppermute x3, waiting for transfers between devices, partner_2(): lax.ppermute(x, axis, [(i, i ^ 1 << apart) for i in range(lax.axis_size(a...  43.7 us
    psum x1, blocking collectives, body(): column_sum = lax.psum(jnp.sum(right_factor * right_factor, axis=0), 'cols')  40.6 us
    another operation x3, other arithmetic, apply_factor(): return jax.scipy.linalg.solve_triangular(low_factor, matrix.T, lower=True).T  39.4 us
  transfers between devices with their start and end apart: 5, of which 5 were waited for; matrix products, arithmetic and copies ran while one was open for 1% of the time, Pallas kernels for 0%

commit v1 on v0

v1 whole, which is shorter than its diff:
```python
import functools

import jax
import jax.numpy as jnp
from jax import lax
from jax.experimental import pallas as pl
from jax.experimental.pallas import tpu as pltpu
from jax.sharding import PartitionSpec as P

ROWS = 8192
COLS = 26624
RANK = 512
feedback_rate = 0.05
epsilon = 1e-05

R = 1024
C = 1664
B = 128
MESH = pl.DeviceIdType.MESH
f32 = jnp.float32
bf16 = jnp.bfloat16
NN = (((1,), (0,)), ((), ()))
NT = (((1,), (1,)), ((), ()))


def mm(a, b, dims):
    return lax.dot_general(a, b, dims, preferred_element_type=f32)


def mm6(a, b, dims):
    return lax.dot_general(a, b, dims, precision=lax.Precision.HIGHEST, preferred_element_type=f32)


def split(a):
    hi = a.astype(bf16)
    return hi, (a - hi.astype(f32)).astype(bf16)


def mm3(a, b, dims):
    return mm(a[0], b[0], dims) + (mm(a[0], b[1], dims) + mm(a[1], b[0], dims))


def tree(terms):
    while len(terms) > 1:
        terms = [a + b for a, b in zip(terms[::2], terms[1::2])]
    return terms[0]


def inverse_factor(block):
    lane = lax.broadcasted_iota(jnp.int32, (8, B), 1)
    sub = lax.broadcasted_iota(jnp.int32, (8, B), 0)
    rows = [block[8 * v : 8 * v + 8, :] for v in range(16)]

    def row(x, l):
        return jnp.broadcast_to(x[l : l + 1, :], (8, B))

    def column(x, l):
        return jnp.broadcast_to(x[:, l : l + 1], (8, B))

    out = []
    for g in range(16):
        o = 8 * g
        active = (lane >= o) & (lane < o + 8)
        c = [column(rows[g], o + m) for m in range(8)]
        e = jnp.where(active, jnp.where(lane - o == sub, 1.0, 0.0), rows[g])
        e_row = [row(e, m) for m in range(8)]
        low = [jnp.where(sub == m, 1.0, 0.0) for m in range(8)]
        pivots = jnp.ones((8, B), f32)
        for l in range(8):
            here = sub == l
            r = [row(c[m], l) for m in range(8)]
            inverse = 1.0 / r[l]
            pivots = jnp.where(here, c[l], pivots)
            for m in range(l):
                low[m] = jnp.where(here, c[m], low[m])
            factor = jnp.where(here, -1.0, c[l])
            for m in range(8):
                if m != l:
                    c[m] = jnp.where(here, 0.0, c[m]) - (factor * r[m]) * inverse
            c[l] = -(factor * inverse)
        t = tree([low[m] * e_row[m] for m in range(8)])
        out.append(lax.rsqrt(pivots) * jnp.where(lane < o + 8, t, 0.0))
        if g == 15:
            break
        w = tree([c[m] * e_row[m] for m in range(8)])
        w_row = [row(w, m) for m in range(8)]
        for v in range(g + 1, 16):
            step = tree([column(rows[v], o + m) * w_row[m] for m in range(8)])
            rows[v] = jnp.where(active, 0.0, rows[v]) - step
    return jnp.concatenate(out, axis=0)


def factor_step(k, gram, inv):
    o, p = B * k, B * (k + 1)
    diagonal = inverse_factor(gram[o:p, o:p])
    if k > 0:
        inv[o:p, 0:o] = mm6(diagonal, inv[o:p, 0:o], NN)
    inv[o:p, o:p] = diagonal
    if k < 3:
        low = mm6(gram[p:, o:p], diagonal, NT)
        gram[p:, p:] = gram[p:, p:] - mm6(low, low, NT)
        inv[p:, 0:p] = inv[p:, 0:p] - mm6(low, inv[o:p, 0:p], NN)


P1, P2, P3, P4 = 0, 6, 12, 18
G0, G1, G2, G3 = 24, 25, 28, 31
W0, W1, W2, W3 = 32, 33, 36, 39
S1, S2 = 40, 43
N_MSG = 46


def sum_kernel(
    mom_hbm, grad_hbm, q_ref,
    p_ref, inv_ref, rt_ref, scale_ref,
    mom, grad, hi, lo, part, recv1, mid, recv2, pt_hi, pt_lo,
    gram, g_recv0, g_recv1, wt, w_recv0, w_recv1, w_sum, col, col_recv,
    load_sem, send_sem, recv_sem,
):
    row, column = lax.axis_index("rows"), lax.axis_index("cols")
    x, core = row // 2, row % 2
    y, z = column // 4, column % 4

    def at_x(d):
        return (((x + d) % 4) * 2 + core, column)

    def at_y(d):
        return (row, ((y + d) % 4) * 4 + z)

    def at_z(d):
        return (row, y * 4 + (z + d) % 4)

    other_core = (x * 2 + 1 - core, column)

    loads = []
    for i in range(4):
        rows = pl.ds(256 * i, 256)
        pair = [
            pltpu.make_async_copy(mom_hbm.at[rows], mom.at[rows], load_sem.at[2 * i]),
            pltpu.make_async_copy(grad_hbm.at[rows], grad.at[rows], load_sem.at[2 * i + 1]),
        ]
        for copy in pair:
            copy.start()
        loads.append(pair)

    barrier = pltpu.get_barrier_semaphore()
    peers = [f(d) for f in (at_x, at_y, at_z) for d in (1, 2, 3)] + [other_core]
    for peer in peers:
        pl.semaphore_signal(barrier, inc=1, device_id=peer, device_id_type=MESH)
    pl.semaphore_wait(barrier, len(peers))

    def send(number, src, dst, peer):
        copy = pltpu.make_async_remote_copy(
            src_ref=src, dst_ref=dst, send_sem=send_sem.at[number], recv_sem=recv_sem.at[number],
            device_id=peer, device_id_type=MESH,
        )
        copy.start()
        return copy

    started = []

    def finish(copies):
        for copy in copies:
            copy.wait_recv()
        started.extend(copies)

    for i in range(4):
        for copy in loads[i]:
            copy.wait()

        @pl.loop(0, 8)
        def _(j):
            rows = pl.ds(pl.multiple_of(256 * i + 32 * j, 32), 32)
            top, rest = split(mom[rows, :] + grad[rows, :].astype(f32))
            hi[rows, :] = top
            lo[rows, :] = rest

    def at_first(h):
        return at_y if h == 0 else at_z

    def at_second(h):
        return at_z if h == 0 else at_y

    first, second = (y, z), (z, y)

    copies = []
    for d in (2, 1, 3, 0):
        for h in range(2):
            block = (first[h] + d) % 4
            rows = pl.ds(pl.multiple_of(block * 256, 256), 256)
            qh = q_ref[:, 256 * h : 256 * h + 256]
            part[h, rows, :] = mm(hi[rows, :], qh, NN) + mm(lo[rows, :], qh, NN)
            if d:
                copies.append(
                    send(P1 + 3 * h + d - 1, part.at[h, rows], recv1.at[h, d - 1], at_first(h)(d))
                )
    finish(copies)
    copies = []
    for h in range(2):
        rows = pl.ds(pl.multiple_of(first[h] * 256, 256), 256)
        mid[h] = (part[h, rows, :] + recv1[h, 0]) + (recv1[h, 1] + recv1[h, 2])
        for d in (2, 1, 3):
            rows = pl.ds(pl.multiple_of(((second[h] + d) % 4) * 64, 64), 64)
            copies.append(
                send(P2 + 3 * h + d - 1, mid.at[h, rows], recv2.at[h, d - 1], at_second(h)(d))
            )
    finish(copies)
    copies = []
    for h in range(2):
        rows = pl.ds(pl.multiple_of(second[h] * 64, 64), 64)
        mine = pl.ds(pl.multiple_of(first[h] * 256 + second[h] * 64, 64), 64)
        p_ref[h, mine, :] = (mid[h, rows, :] + recv2[h, 0]) + (recv2[h, 1] + recv2[h, 2])
        for d in (2, 1, 3):
            copies.append(
                send(P3 + 3 * h + d - 1, p_ref.at[h, mine], p_ref.at[h, mine], at_second(h)(d))
            )
    finish(copies)
    copies = []
    for h in range(2):
        mine = pl.ds(pl.multiple_of(first[h] * 256, 256), 256)
        for d in (2, 1, 3):
            copies.append(
                send(P4 + 3 * h + d - 1, p_ref.at[h, mine], p_ref.at[h, mine], at_first(h)(d))
            )
    finish(copies)

    for h in range(2):
        for i in range(4):
            t = p_ref[h, 256 * i : 256 * i + 256, :].T
            top, rest = split(t)
            pt_hi[256 * h : 256 * h + 256, 256 * i : 256 * i + 256] = top
            pt_lo[256 * h : 256 * h + 256, 256 * i : 256 * i + 256] = rest
    gram[...] = mm(pt_lo[...], pt_lo[...], NT) + mm3(
        (pt_hi[...], pt_lo[...]), (pt_hi[...], pt_lo[...]), NT
    )
    ours = pl.ds(pl.multiple_of(core * 256, 256), 256)
    theirs = pl.ds(pl.multiple_of((1 - core) * 256, 256), 256)
    g0 = send(G0, gram.at[theirs], g_recv0, other_core)

    def product(half):
        @pl.loop(0, 2)
        def _(j):
            rows = pl.ds(pl.multiple_of(half * 256 + 128 * j, 128), 128)
            wt[rows, :] = mm3((pt_hi[rows, :], pt_lo[rows, :]), (hi[...], lo[...]), NN)

    product(1 - core)
    w0 = send(W0, wt.at[theirs], w_recv0, other_core)
    finish([g0])
    gram[ours, :] = gram[ours, :] + g_recv0[...]

    def slab(i):
        return pl.ds(pl.multiple_of(core * 256 + i * 64, 64), 64)

    g1 = [send(G1 + d - 1, gram.at[slab((x + d) % 4)], g_recv1.at[d - 1], at_x(d)) for d in (2, 1, 3)]
    product(core)
    finish(g1)
    mine = slab(x)
    inv_ref[mine, :] = (gram[mine, :] + g_recv1[0]) + (g_recv1[1] + g_recv1[2])
    g2 = [send(G2 + d - 1, inv_ref.at[mine], inv_ref.at[mine], at_x(d)) for d in (2, 1, 3)]
    finish([w0])
    wt[ours, :] = wt[ours, :] + w_recv0[...]
    finish(g2)
    g3 = send(G3, inv_ref.at[ours], inv_ref.at[ours], other_core)
    w1 = [send(W1 + d - 1, wt.at[slab((x + d) % 4)], w_recv1.at[d - 1], at_x(d)) for d in (2, 1, 3)]
    finish([g3])
    settled = [g0, g3] + g1 + g2
    for copy in settled:
        copy.wait_send()

    gram[...] = inv_ref[...]
    inv_ref[...] = jnp.zeros((RANK, RANK), f32)
    factor_step(0, gram, inv_ref)
    factor_step(1, gram, inv_ref)
    finish(w1)
    w_sum[mine, :] = (wt[mine, :] + w_recv1[0]) + (w_recv1[1] + w_recv1[2])
    w2 = [send(W2 + d - 1, w_sum.at[mine], w_sum.at[mine], at_x(d)) for d in (2, 1, 3)]
    factor_step(2, gram, inv_ref)
    factor_step(3, gram, inv_ref)
    finish(w2)
    w3 = send(W3, w_sum.at[ours], w_sum.at[ours], other_core)
    finish([w3])

    inv_pair = split(inv_ref[...])
    squares = jnp.zeros((RANK, B), f32)
    for j in range(13):
        lanes = slice(B * j, B * j + B)
        r = mm3(inv_pair, split(w_sum[:, lanes]), NN)
        rt_ref[:, lanes] = r
        squares = squares + r * r
    col[0] = mm6(jnp.ones((8, B), f32), squares, NT)
    copies = [send(S1 + d - 1, col.at[0], col_recv.at[0, d - 1], at_y(d)) for d in (2, 1, 3)]
    finish(copies)
    col[1] = (col[0] + col_recv[0, 0]) + (col_recv[0, 1] + col_recv[0, 2])
    copies = [send(S2 + d - 1, col.at[1], col_recv.at[1, d - 1], at_z(d)) for d in (2, 1, 3)]
    finish(copies)
    total = (col[1] + col_recv[1, 0]) + (col_recv[1, 1] + col_recv[1, 2])
    scale_ref[...] = lax.rsqrt(total * (1.0 / COLS) + epsilon)
    for copy in started:
        if not any(copy is other for other in settled):
            copy.wait_send()


def sums(momentum, grad, q_basis):
    vmem = pl.BlockSpec(memory_space=pltpu.VMEM)
    hbm = pl.BlockSpec(memory_space=pl.ANY)
    return pl.pallas_call(
        sum_kernel,
        out_shape=[
            jax.ShapeDtypeStruct((2, R, 256), f32),
            jax.ShapeDtypeStruct((RANK, RANK), f32),
            jax.ShapeDtypeStruct((RANK, C), f32),
            jax.ShapeDtypeStruct((8, RANK), f32),
        ],
        in_specs=[hbm, hbm, vmem],
        out_specs=[vmem] * 4,
        scratch_shapes=[
            pltpu.VMEM((R, C), f32),
            pltpu.VMEM((R, C), bf16),
            pltpu.VMEM((R, C), bf16),
            pltpu.VMEM((R, C), bf16),
            pltpu.VMEM((2, R, 256), f32),
            pltpu.VMEM((2, 3, 256, 256), f32),
            pltpu.VMEM((2, 256, 256), f32),
            pltpu.VMEM((2, 3, 64, 256), f32),
            pltpu.VMEM((RANK, R), bf16),
            pltpu.VMEM((RANK, R), bf16),
            pltpu.VMEM((RANK, RANK), f32),
            pltpu.VMEM((256, RANK), f32),
            pltpu.VMEM((3, 64, RANK), f32),
            pltpu.VMEM((RANK, C), f32),
            pltpu.VMEM((256, C), f32),
            pltpu.VMEM((3, 64, C), f32),
            pltpu.VMEM((RANK, C), f32),
            pltpu.VMEM((2, 8, RANK), f32),
            pltpu.VMEM((2, 3, 8, RANK), f32),
            pltpu.SemaphoreType.DMA((8,)),
            pltpu.SemaphoreType.DMA((N_MSG,)),
            pltpu.SemaphoreType.DMA((N_MSG,)),
        ],
        compiler_params=pltpu.CompilerParams(
            collective_id=0, has_side_effects=True, vmem_limit_bytes=58 << 20
        ),
        name="sums",
    )(momentum, grad, q_basis)


def output_kernel(mom, grad, p_ref, inv_ref, rt_ref, scale_ref, mom_out, q_out, update_out, r_hi, r_lo, i_hi, i_lo):
    scale = scale_ref[0:1, :]

    @pl.when(pl.program_id(0) == 0)
    def _():
        i_hi[...], i_lo[...] = split(inv_ref[...])
        for j in range(13):
            lanes = slice(B * j, B * j + B)
            r = rt_ref[:, lanes]
            r_hi[:, lanes], r_lo[:, lanes] = split(r)
            q_out[lanes, :] = (r.T * scale).astype(bf16)

    p = jnp.concatenate([p_ref[0], p_ref[1]], axis=1)
    orth = mm3(split(p), (i_hi[...], i_lo[...]), NT)
    orth_hi = (orth * feedback_rate).astype(bf16)
    scaled = split(orth * (scale * (float(ROWS) / RANK) ** 0.5))
    mom_out[...] = mom[...] + grad[...].astype(f32) - mm(orth_hi, r_hi[...], NN)
    update_out[...] = mm3(scaled, (r_hi[...], r_lo[...]), NN).astype(bf16)


def outputs(momentum, grad, p, inv, rt, scale):
    rows = 128
    whole = lambda *shape: pl.BlockSpec(shape, lambda i: (0,) * len(shape))
    slab = pl.BlockSpec((rows, C), lambda i: (i, 0))
    return pl.pallas_call(
        output_kernel,
        grid=(R // rows,),
        out_shape=[
            jax.ShapeDtypeStruct((R, C), f32),
            jax.ShapeDtypeStruct((C, RANK), bf16),
            jax.ShapeDtypeStruct((R, C), bf16),
        ],
        in_specs=[
            slab, slab, pl.BlockSpec((2, rows, 256), lambda i: (0, i, 0)),
            whole(RANK, RANK), whole(RANK, C), whole(8, RANK),
        ],
        out_specs=[slab, whole(C, RANK), slab],
        scratch_shapes=[
            pltpu.VMEM((RANK, C), bf16),
            pltpu.VMEM((RANK, C), bf16),
            pltpu.VMEM((RANK, RANK), bf16),
            pltpu.VMEM((RANK, RANK), bf16),
        ],
        compiler_params=pltpu.CompilerParams(vmem_limit_bytes=50 << 20),
        name="outputs",
    )(momentum, grad, p, inv, rt, scale)


def body(momentum, grad, q_basis):
    p, inv, rt, scale = sums(momentum, grad, q_basis)
    return tuple(outputs(momentum, grad, p, inv, rt, scale))


def solution(mesh):
    return jax.shard_map(
        body,
        mesh=mesh,
        in_specs=(P("rows", "cols"), P("rows", "cols"), P("cols", None)),
        out_specs=(P("rows", "cols"), P("cols", None), P("rows", "cols")),
        check_vma=False,
    )
```

time: 800 us -> 153 us (0.19)
  other arithmetic: 364 us -> 0 us
  waiting for transfers between devices: 206 us -> 0 us
  Pallas kernels: 0 us -> 147 us
  matrix products: 141 us -> 0 us
  blocking collectives: 40.6 us -> 0 us
  between operations: 25.6 us -> 0.7 us
  local copies, waits for them, and re-layouts: 15.1 us -> 3.53 us
    another operation x62 -> x0, other arithmetic: 356 us -> none  [the longest x45 238 us: body(): jnp.linalg.cholesky(exact_dot(low_factor, low_factor.T) + exact_dot(partn...]
    psum x2 -> x0, waiting for transfers between devices: 162 us -> none  [the longest x1 92.8 us: body(): projected = lax.psum(exact_dot(merged, q_float_in), 'cols')]
    pallas_call x0 -> x2, Pallas kernels: none -> 147 us  [the longest x1 128 us: sums(): pl.pallas_call(sum_kernel, out_shape=[jax.ShapeDtypeStruct((2, R, 256), f...]
    dot_general x11 -> x0, matrix products: 106 us -> none  [the longest x9 73.3 us: exact_dot(): jnp.dot(left, right_side, precision=lax.Precision.HIGHEST, preferred_elem...]
    ppermute x3 -> x0, waiting for transfers between devices: 43.7 us -> none  [partner_2(): lax.ppermute(x, axis, [(i, i ^ 1 << apart) for i in range(lax.axis_size(a...]
    psum x1 -> x0, blocking collectives: 40.6 us -> none  [body(): column_sum = lax.psum(jnp.sum(right_factor * right_factor, axis=0), 'cols')]
    another operation x31 -> x0, matrix products: 34.6 us -> none  [the longest x18 16.6 us: body(): jnp.linalg.cholesky(exact_dot(low_factor, low_factor.T) + exact_dot(partn...]
    another operation x29 -> x0, local copies, waits for them, and re-layouts: 8.49 us -> none
  transfers between devices with their start and end apart: 5 -> 0, of which waited for: 5 -> 0; matrix products, arithmetic and copies ran while one was open for 1% -> 0% of each run, Pallas kernels for 0% -> 0%
where the time goes in v1:
time: 153 us; the launch traced here: 151 us
  Pallas kernels  147 us (96%)
  local copies, waits for them, and re-layouts  3.53 us (2%)
    pallas_call x1, Pallas kernels, sums(): pl.pallas_call(sum_kernel, out_shape=[jax.ShapeDtypeStruct((2, R, 256), f...  128 us
    pallas_call x1, Pallas kernels, outputs(): pl.pallas_call(output_kernel, grid=(R // rows,), out_shape=[jax.ShapeDtyp...  18.7 us
    unnamed x6, local copies, waits for them, and re-layouts  3.53 us

profile of v1, /device:TPU:0, one launch (start us, length us, event | category | flops | bytes accessed | tf_op | source)
XLA Modules:
  0.0 151.3 jit_solution(7228975083052638021)
XLA Ops:
  0.6 128.4 %sums.1 = (f32[2,1024,256]{2,1,0:T(8,128)}, f32[512,512]{1,0:T(8,128)}, f32[512,1664]{1,0:T(8,128)}, f32[8,512]{1,0:T(8,128)}) custom-call(f32[1024,1664]{1,0:T(8,128)} %mom.1, bf16[1024,1664]{1,0:T(8,128)(2,1)} %grad.1, bf16[1664,512]{1,0:T(8,128)(2,1)} %q_ref.1), custom_call_target="tpu_custom_call" | custom-call | tf_op jit(solution)/shard_map/sums/pallas_call | solution.py:305
  129.0 0.0 copy-start
  129.0 1.6 %copy-done = f32[2,1024,256]{2,1,0:T(8,128)S(1)} copy-done((f32[2,1024,256]{2,1,0:T(8,128)S(1)}, f32[2,1024,256]{2,1,0:T(8,128)}, u32[]{:S(2)}) %copy-start) | copy-done | bytes 2097176
  130.6 0.0 copy-start.1
  130.6 1.2 copy-done.1
  131.8 0.0 copy-start.2
  131.8 0.7 copy-done.2
  132.5 18.7 %outputs.1 = (f32[1024,1664]{1,0:T(8,128)}, bf16[1664,512]{1,0:T(8,128)(2,1)}, bf16[1024,1664]{1,0:T(8,128)(2,1)}) custom-call(f32[1024,1664]{1,0:T(8,128)} %mom.1, bf16[1024,1664]{1,0:T(8,128)(2,1)} %grad.1, f32[2,1024,256]{2,1,0:T(8,128)S(1)} %copy-done, f32[512,512]{1,0:T(8,128)S(1)} %copy-done.1, f32[512,1664]{1,0:T(8,128)} %get-tuple-element.9.rt_ref, ...), custom_call_target="tpu_custom_call" | custom-call | tf_op jit(solution)/shard_map/outputs/pallas_call | solution.py:370
Async XLA Ops:
  129.0 1.6 %copy-start = (f32[2,1024,256]{2,1,0:T(8,128)S(1)}, f32[2,1024,256]{2,1,0:T(8,128)}, u32[]{:S(2)}) copy-start(f32[2,1024,256]{2,1,0:T(8,128)} %get-tuple-element.7.p_ref) | copy-start | bytes 6291460
  130.6 1.2 copy-start.1
  131.8 0.7 copy-start.2

commit v2 on v1

v2 whole, which is shorter than its diff:
```python
import functools

import jax
import jax.numpy as jnp
from jax import lax
from jax.experimental import pallas as pl
from jax.experimental.pallas import tpu as pltpu
from jax.sharding import PartitionSpec as P

ROWS = 8192
COLS = 26624
RANK = 512
feedback_rate = 0.05
epsilon = 1e-05

R = 1024
C = 1664
B = 128
MESH = pl.DeviceIdType.MESH
f32 = jnp.float32
bf16 = jnp.bfloat16
NN = (((1,), (0,)), ((), ()))
NT = (((1,), (1,)), ((), ()))


def mm(a, b, dims):
    return lax.dot_general(a, b, dims, preferred_element_type=f32)


def mm6(a, b, dims):
    return lax.dot_general(a, b, dims, precision=lax.Precision.HIGHEST, preferred_element_type=f32)


def split(a):
    hi = a.astype(bf16)
    return hi, (a - hi.astype(f32)).astype(bf16)


def mm3(a, b, dims):
    return mm(a[0], b[0], dims) + (mm(a[0], b[1], dims) + mm(a[1], b[0], dims))


def tree(terms):
    while len(terms) > 1:
        terms = [a + b for a, b in zip(terms[::2], terms[1::2])]
    return terms[0]


def inverse_factor(block):
    lane = lax.broadcasted_iota(jnp.int32, (8, B), 1)
    sub = lax.broadcasted_iota(jnp.int32, (8, B), 0)
    rows = [block[8 * v : 8 * v + 8, :] for v in range(16)]

    def row(x, l):
        return jnp.broadcast_to(x[l : l + 1, :], (8, B))

    def column(x, l):
        return jnp.broadcast_to(x[:, l : l + 1], (8, B))

    out = []
    for g in range(16):
        o = 8 * g
        active = (lane >= o) & (lane < o + 8)
        c = [column(rows[g], o + m) for m in range(8)]
        e = jnp.where(active, jnp.where(lane - o == sub, 1.0, 0.0), rows[g])
        e_row = [row(e, m) for m in range(8)]
        low = [jnp.where(sub == m, 1.0, 0.0) for m in range(8)]
        pivots = jnp.ones((8, B), f32)
        for l in range(8):
            here = sub == l
            r = [row(c[m], l) for m in range(8)]
            inverse = 1.0 / r[l]
            pivots = jnp.where(here, c[l], pivots)
            for m in range(l):
                low[m] = jnp.where(here, c[m], low[m])
            factor = jnp.where(here, -1.0, c[l])
            for m in range(8):
                if m != l:
                    c[m] = jnp.where(here, 0.0, c[m]) - (factor * r[m]) * inverse
            c[l] = -(factor * inverse)
        t = tree([low[m] * e_row[m] for m in range(8)])
        out.append(lax.rsqrt(pivots) * jnp.where(lane < o + 8, t, 0.0))
        if g == 15:
            break
        w = tree([c[m] * e_row[m] for m in range(8)])
        w_row = [row(w, m) for m in range(8)]
        for v in range(g + 1, 16):
            step = tree([column(rows[v], o + m) * w_row[m] for m in range(8)])
            rows[v] = jnp.where(active, 0.0, rows[v]) - step
    return jnp.concatenate(out, axis=0)


def factor_step(k, gram, inv):
    o, p = B * k, B * (k + 1)
    diagonal = inverse_factor(gram[o:p, o:p])
    if k > 0:
        inv[o:p, 0:o] = mm6(diagonal, inv[o:p, 0:o], NN)
    inv[o:p, o:p] = diagonal
    if k < 3:
        low = mm6(gram[p:, o:p], diagonal, NT)
        gram[p:, p:] = gram[p:, p:] - mm6(low, low, NT)
        inv[p:, 0:p] = inv[p:, 0:p] - mm6(low, inv[o:p, 0:p], NN)


PACKED = [(0, 0), (1, 0), (1, 1), (2, 0), (2, 1), (2, 2), (3, 0), (3, 1), (3, 2), (3, 3)]
LANES = [(256 * j, min(256, C - 256 * j)) for j in range(7)]
N_MSG = 78


def sum_kernel(
    mom_hbm, grad_hbm, q_ref,
    orth_hbm, r_hi_hbm, r_lo_hbm, right_hbm, scale_ref,
    mom, grad, hi, lo, part, recv1, mid, recv2, p_buf, pt_hi, pt_lo,
    packed, g_recv0, g_recv1, g_sum, gram, inv, wt, w_recv0, w_recv1, w_sum,
    orth, r_hi, r_lo, right, col, col_recv,
    load_sem, save_sem, send_sem, recv_sem,
):
    row, column = lax.axis_index("rows"), lax.axis_index("cols")
    x, core = row // 2, row % 2
    y, z = column // 4, column % 4

    def at_x(d):
        return (((x + d) % 4) * 2 + core, column)

    def at_y(d):
        return (row, ((y + d) % 4) * 4 + z)

    def at_z(d):
        return (row, y * 4 + (z + d) % 4)

    other_core = (x * 2 + 1 - core, column)

    def block(start, size):
        return pl.ds(pl.multiple_of(start, size), size)

    loads = []
    for i in range(4):
        rows = pl.ds(256 * i, 256)
        pair = [
            pltpu.make_async_copy(mom_hbm.at[rows], mom.at[rows], load_sem.at[2 * i]),
            pltpu.make_async_copy(grad_hbm.at[rows], grad.at[rows], load_sem.at[2 * i + 1]),
        ]
        for copy in pair:
            copy.start()
        loads.append(pair)

    barrier = pltpu.get_barrier_semaphore()
    peers = [f(d) for f in (at_x, at_y, at_z) for d in (1, 2, 3)] + [other_core]
    for peer in peers:
        pl.semaphore_signal(barrier, inc=1, device_id=peer, device_id_type=MESH)
    pl.semaphore_wait(barrier, len(peers))

    started = []

    def send(src, dst, peer):
        number = len(started)
        copy = pltpu.make_async_remote_copy(
            src_ref=src, dst_ref=dst, send_sem=send_sem.at[number], recv_sem=recv_sem.at[number],
            device_id=peer, device_id_type=MESH,
        )
        copy.start()
        started.append(copy)
        return copy

    def finish(copies):
        for copy in copies:
            copy.wait_recv()

    at_first, at_second = (at_y, at_z), (at_z, at_y)
    first, second = (y, z), (z, y)
    groups = lambda s: [(2 * s + h, h) for h in range(2)]

    def product_p(s, i):
        rows = pl.ds(256 * i, 256)
        q = q_ref[:, 256 * s : 256 * s + 256]
        value = mm(hi[rows, :], q, NN) + mm(lo[rows, :], q, NN)
        part[2 * s, rows, :] = value[:, :B]
        part[2 * s + 1, rows, :] = value[:, B:]

    def scatter_first(s):
        copies = []
        for d in (2, 1, 3):
            for k, h in groups(s):
                rows = block(((first[h] + d) % 4) * 256, 256)
                copies.append(send(part.at[k, rows], recv1.at[k, d - 1], at_first[h](d)))
        return copies

    def scatter_second(s):
        copies = []
        for k, h in groups(s):
            rows = block(first[h] * 256, 256)
            mid[k] = (part[k, rows, :] + recv1[k, 0]) + (recv1[k, 1] + recv1[k, 2])
            for d in (2, 1, 3):
                rows = block(((second[h] + d) % 4) * 64, 64)
                copies.append(send(mid.at[k, rows], recv2.at[k, d - 1], at_second[h](d)))
        return copies

    def gather_second(s):
        copies = []
        for k, h in groups(s):
            rows = block(second[h] * 64, 64)
            mine = block(first[h] * 256 + second[h] * 64, 64)
            p_buf[k, mine, :] = (mid[k, rows, :] + recv2[k, 0]) + (recv2[k, 1] + recv2[k, 2])
            for d in (2, 1, 3):
                copies.append(send(p_buf.at[k, mine], p_buf.at[k, mine], at_second[h](d)))
        return copies

    def gather_first(s):
        copies = []
        for k, h in groups(s):
            mine = block(first[h] * 256, 256)
            for d in (2, 1, 3):
                copies.append(send(p_buf.at[k, mine], p_buf.at[k, mine], at_first[h](d)))
        return copies

    for i in range(4):
        for copy in loads[i]:
            copy.wait()

        @pl.loop(0, 8)
        def _(j):
            rows = block(256 * i + 32 * j, 32)
            top, rest = split(mom[rows, :] + grad[rows, :].astype(f32))
            hi[rows, :] = top
            lo[rows, :] = rest

        product_p(0, i)
    p1_0 = scatter_first(0)
    for i in range(4):
        product_p(1, i)
    p1_1 = scatter_first(1)
    finish(p1_0)
    p2_0 = scatter_second(0)
    finish(p1_1)
    p2_1 = scatter_second(1)
    finish(p2_0)
    p3_0 = gather_second(0)
    finish(p2_1)
    p3_1 = gather_second(1)
    finish(p3_0)
    p4_0 = gather_first(0)
    finish(p3_1)
    p4_1 = gather_first(1)

    def transpose_p(s):
        for k, _ in groups(s):
            for i in range(4):
                rows = slice(256 * i, 256 * i + 256)
                top, rest = split(p_buf[k, rows, :].T)
                pt_hi[B * k : B * k + B, rows] = top
                pt_lo[B * k : B * k + B, rows] = rest

    def gram_block(s, t):
        a, b = slice(256 * s, 256 * s + 256), slice(256 * t, 256 * t + 256)
        value = mm(pt_lo[a, :], pt_lo[b, :], NT) + mm3((pt_hi[a, :], pt_lo[a, :]), (pt_hi[b, :], pt_lo[b, :]), NT)
        for n, (i, j) in enumerate(PACKED):
            if i // 2 == s and j // 2 == t:
                r, c = B * (i % 2), B * (j % 2)
                packed[B * n : B * n + B, :] = value[r : r + B, c : c + B]

    def product_w(s):
        rows = slice(256 * s, 256 * s + 256)

        def chunk(lanes):
            wt[rows, lanes] = mm3((pt_hi[rows, :], pt_lo[rows, :]), (hi[:, lanes], lo[:, lanes]), NN)

        @pl.loop(0, 6)
        def _(j):
            chunk(block(256 * j, 256))

        chunk(slice(1536, 1664))

    def ours(s):
        return block(256 * s + B * core, B)

    def theirs(s):
        return block(256 * s + B * (1 - core), B)

    def slab(s, i):
        return block(256 * s + B * core + 32 * i, 32)

    def w_cores(s):
        return [send(wt.at[theirs(s)], w_recv0.at[s], other_core)]

    def w_scatter(s):
        wt[ours(s), :] = wt[ours(s), :] + w_recv0[s]
        return [send(wt.at[slab(s, (x + d) % 4)], w_recv1.at[s, d - 1], at_x(d)) for d in (2, 1, 3)]

    def w_gather(s):
        mine = slab(s, x)
        w_sum[mine, :] = (wt[mine, :] + w_recv1[s, 0]) + (w_recv1[s, 1] + w_recv1[s, 2])
        return [send(w_sum.at[mine], w_sum.at[mine], at_x(d)) for d in (2, 1, 3)]

    def w_back(s):
        return [send(w_sum.at[ours(s)], w_sum.at[ours(s)], other_core)]

    finish(p4_0)
    transpose_p(0)
    product_w(0)
    w0_0 = w_cores(0)
    gram_block(0, 0)
    finish(w0_0)
    w1_0 = w_scatter(0)
    finish(p4_1)
    transpose_p(1)
    gram_block(1, 0)
    gram_block(1, 1)
    g_ours, g_theirs = block(640 * core, 640), block(640 * (1 - core), 640)
    g0 = [send(packed.at[g_theirs], g_recv0, other_core)]
    product_w(1)
    w0_1 = w_cores(1)
    finish(g0)
    packed[g_ours, :] = packed[g_ours, :] + g_recv0[...]

    def g_slab(i):
        return block(640 * core + 160 * i, 160)

    g1 = [send(packed.at[g_slab((x + d) % 4)], g_recv1.at[d - 1], at_x(d)) for d in (2, 1, 3)]
    finish(w0_1)
    finish(g1)
    g_mine = g_slab(x)
    g_sum[g_mine, :] = (packed[g_mine, :] + g_recv1[0]) + (g_recv1[1] + g_recv1[2])
    g2 = [send(g_sum.at[g_mine], g_sum.at[g_mine], at_x(d)) for d in (2, 1, 3)]
    w1_1 = w_scatter(1)
    finish(w1_0)
    w2_0 = w_gather(0)
    finish(g2)
    g3 = [send(g_sum.at[g_ours], g_sum.at[g_ours], other_core)]
    inv[...] = jnp.zeros((RANK, RANK), f32)
    finish(g3)
    for n, (i, j) in enumerate(PACKED):
        gram[B * i : B * i + B, B * j : B * j + B] = g_sum[B * n : B * n + B, :]

    factor_step(0, gram, inv)
    finish(w1_1)
    w2_1 = w_gather(1)
    factor_step(1, gram, inv)
    factor_step(2, gram, inv)
    finish(w2_0)
    w3_0 = w_back(0)
    factor_step(3, gram, inv)
    finish(w2_1)
    w3_1 = w_back(1)
    finish(w3_0 + w3_1)

    inv_hi, inv_lo = split(inv[...])
    squares = jnp.zeros((RANK, B), f32)
    for start, size in LANES:
        lanes = slice(start, start + size)
        w = split(w_sum[:, lanes])
        top = mm3((inv_hi[:256, :256], inv_lo[:256, :256]), (w[0][:256], w[1][:256]), NN)
        bottom = mm3((inv_hi[256:], inv_lo[256:]), w, NN)
        r = jnp.concatenate([top, bottom], axis=0)
        mom[0:RANK, lanes] = r
        r_hi[:, lanes], r_lo[:, lanes] = split(r)
        for i in range(0, size, B):
            squares = squares + r[:, i : i + B] * r[:, i : i + B]
    saves = []

    def save(src, dst):
        copy = pltpu.make_async_copy(src, dst, save_sem.at[len(saves)])
        copy.start()
        saves.append(copy)

    save(r_hi, r_hi_hbm)
    save(r_lo, r_lo_hbm)
    col[0] = mm6(jnp.ones((8, B), f32), squares, NT)
    s1 = [send(col.at[0], col_recv.at[0, d - 1], at_y(d)) for d in (2, 1, 3)]
    for i in range(4):
        rows = slice(256 * i, 256 * i + 256)
        p = split(jnp.concatenate([p_buf[k, rows, :] for k in range(4)], axis=1))
        orth[rows, :] = mm3(p, (inv_hi, inv_lo), NT)
    save(orth, orth_hbm)
    finish(s1)
    col[1] = (col[0] + col_recv[0, 0]) + (col_recv[0, 1] + col_recv[0, 2])
    s2 = [send(col.at[1], col_recv.at[1, d - 1], at_z(d)) for d in (2, 1, 3)]
    for j in range(13):
        lanes = slice(B * j, B * j + B)
        right[lanes, :] = mom[0:RANK, lanes].T
    save(right, right_hbm)
    finish(s2)
    total = (col[1] + col_recv[1, 0]) + (col_recv[1, 1] + col_recv[1, 2])
    scale_ref[...] = lax.rsqrt(total * (1.0 / COLS) + epsilon)
    for copy in saves:
        copy.wait()
    for copy in started:
        copy.wait_send()


def sums(momentum, grad, q_basis):
    vmem = pl.BlockSpec(memory_space=pltpu.VMEM)
    hbm = pl.BlockSpec(memory_space=pl.ANY)
    return pl.pallas_call(
        sum_kernel,
        out_shape=[
            jax.ShapeDtypeStruct((R, RANK), f32),
            jax.ShapeDtypeStruct((RANK, C), bf16),
            jax.ShapeDtypeStruct((RANK, C), bf16),
            jax.ShapeDtypeStruct((C, RANK), f32),
            jax.ShapeDtypeStruct((8, RANK), f32),
        ],
        in_specs=[hbm, hbm, vmem],
        out_specs=[hbm] * 4 + [vmem],
        scratch_shapes=[
            pltpu.VMEM((R, C), f32),
            pltpu.VMEM((R, C), bf16),
            pltpu.VMEM((R, C), bf16),
            pltpu.VMEM((R, C), bf16),
            pltpu.VMEM((4, R, B), f32),
            pltpu.VMEM((4, 3, 256, B), f32),
            pltpu.VMEM((4, 256, B), f32),
            pltpu.VMEM((4, 3, 64, B), f32),
            pltpu.VMEM((4, R, B), f32),
            pltpu.VMEM((RANK, R), bf16),
            pltpu.VMEM((RANK, R), bf16),
            pltpu.VMEM((1280, B), f32),
            pltpu.VMEM((640, B), f32),
            pltpu.VMEM((3, 160, B), f32),
            pltpu.VMEM((1280, B), f32),
            pltpu.VMEM((RANK, RANK), f32),
            pltpu.VMEM((RANK, RANK), f32),
            pltpu.VMEM((RANK, C), f32),
            pltpu.VMEM((2, B, C), f32),
            pltpu.VMEM((2, 3, 32, C), f32),
            pltpu.VMEM((RANK, C), f32),
            pltpu.VMEM((R, RANK), f32),
            pltpu.VMEM((RANK, C), bf16),
            pltpu.VMEM((RANK, C), bf16),
            pltpu.VMEM((C, RANK), f32),
            pltpu.VMEM((2, 8, RANK), f32),
            pltpu.VMEM((2, 3, 8, RANK), f32),
            pltpu.SemaphoreType.DMA((8,)),
            pltpu.SemaphoreType.DMA((4,)),
            pltpu.SemaphoreType.DMA((N_MSG,)),
            pltpu.SemaphoreType.DMA((N_MSG,)),
        ],
        compiler_params=pltpu.CompilerParams(
            collective_id=0, has_side_effects=True, vmem_limit_bytes=60 << 20
        ),
        name="sums",
    )(momentum, grad, q_basis)


def output_kernel(mom, grad, orth_ref, r_hi, r_lo, right, scale_ref, mom_out, q_out, update_out):
    scale = scale_ref[0:1, :]
    q_out[...] = (right[...] * scale).astype(bf16)
    orth = orth_ref[...]
    scaled = split(orth * (scale * (float(ROWS) / RANK) ** 0.5))
    step = (orth * feedback_rate).astype(bf16)
    for start, size in LANES:
        lanes = slice(start, start + size)
        top = r_hi[:, lanes]
        merged = mom[:, lanes] + grad[:, lanes].astype(f32)
        mom_out[:, lanes] = merged - mm(step, top, NN)
        update_out[:, lanes] = mm3(scaled, (top, r_lo[:, lanes]), NN).astype(bf16)


def outputs(momentum, grad, orth, r_hi, r_lo, right, scale):
    steps = 4
    rows = R // steps
    whole = lambda *shape: pl.BlockSpec(shape, lambda i: (0,) * len(shape))
    slab = lambda n, width: pl.BlockSpec((n // steps, width), lambda i: (i, 0))
    return pl.pallas_call(
        output_kernel,
        grid=(steps,),
        out_shape=[
            jax.ShapeDtypeStruct((R, C), f32),
            jax.ShapeDtypeStruct((C, RANK), bf16),
            jax.ShapeDtypeStruct((R, C), bf16),
        ],
        in_specs=[
            slab(R, C), slab(R, C), slab(R, RANK), whole(RANK, C), whole(RANK, C), slab(C, RANK), whole(8, RANK),
        ],
        out_specs=[slab(R, C), slab(C, RANK), slab(R, C)],
        compiler_params=pltpu.CompilerParams(vmem_limit_bytes=60 << 20),
        name="outputs",
    )(momentum, grad, orth, r_hi, r_lo, right, scale)


def body(momentum, grad, q_basis):
    return tuple(outputs(momentum, grad, *sums(momentum, grad, q_basis)))


def solution(mesh):
    return jax.shard_map(
        body,
        mesh=mesh,
        in_specs=(P("rows", "cols"), P("rows", "cols"), P("cols", None)),
        out_specs=(P("rows", "cols"), P("cols", None), P("rows", "cols")),
        check_vma=False,
    )
```

time: 153 us -> 128 us (0.84)
  Pallas kernels: 147 us -> 127 us
  local copies, waits for them, and re-layouts: 3.53 us -> 0 us
    pallas_call x2, Pallas kernels: 147 us -> 127 us  [the longest x1 113 us: sums(): pl.pallas_call(sum_kernel, out_shape=[jax.ShapeDtypeStruct((R, RANK), f32...]
    unnamed x6 -> x0, local copies, waits for them, and re-layouts: 3.53 us -> none
where the time goes in v2:
time: 128 us
  Pallas kernels  127 us (99%)
    pallas_call x1, Pallas kernels, sums(): pl.pallas_call(sum_kernel, out_shape=[jax.ShapeDtypeStruct((R, RANK), f32...  113 us
    pallas_call x1, Pallas kernels, outputs(): pl.pallas_call(output_kernel, grid=(steps,), out_shape=[jax.ShapeDtypeStr...  14.2 us

profile of v2, /device:TPU:0, one launch (start us, length us, event | category | flops | bytes accessed | tf_op | source)
XLA Modules:
  0.0 127.5 jit_solution(15571947728989797258)
XLA Ops:
  0.6 112.7 %sums.1 = (f32[1024,512]{1,0:T(8,128)}, bf16[512,1664]{1,0:T(8,128)(2,1)}, bf16[512,1664]{1,0:T(8,128)(2,1)}, f32[1664,512]{1,0:T(8,128)}, f32[8,512]{1,0:T(8,128)}) custom-call(f32[1024,1664]{1,0:T(8,128)} %mom.1, bf16[1024,1664]{1,0:T(8,128)(2,1)} %grad.1, bf16[1664,512]{1,0:T(8,128)(2,1)} %q_ref.1), custom_call_target="tpu_custom_call" | custom-call | tf_op jit(solution)/shard_map/sums/pallas_call | solution.py:393
  113.3 14.2 %outputs.1 = (f32[1024,1664]{1,0:T(8,128)}, bf16[1664,512]{1,0:T(8,128)(2,1)}, bf16[1024,1664]{1,0:T(8,128)(2,1)}) custom-call(f32[1024,1664]{1,0:T(8,128)} %mom.1, bf16[1024,1664]{1,0:T(8,128)(2,1)} %grad.1, f32[1024,512]{1,0:T(8,128)} %get-tuple-element.8.orth_ref, bf16[512,1664]{1,0:T(8,128)(2,1)} %get-tuple-element.9.r_hi, ...), custom_call_target="tpu_custom_call" | custom-call | tf_op jit(solution)/shard_map/outputs/pallas_call | solution.py:463

commit v3 on v2

--- a/solution.py
+++ b/solution.py
@@ -66,18 +66,23 @@
         e_row = [row(e, m) for m in range(8)]
         low = [jnp.where(sub == m, 1.0, 0.0) for m in range(8)]
         pivots = jnp.ones((8, B), f32)
-        for l in range(8):
-            here = sub == l
+        for l in range(0, 8, 2):
+            at0, at1 = sub == l, sub == l + 1
             r = [row(c[m], l) for m in range(8)]
-            inverse = 1.0 / r[l]
-            pivots = jnp.where(here, c[l], pivots)
+            s = [row(c[m], l + 1) for m in range(8)]
+            p, q, t = r[l], r[l + 1], s[l + 1]
+            inverse = 1.0 / (p * t - q * q)
+            ratio = q / p
+            pivots = jnp.where(at0, p, jnp.where(at1, t - ratio * q, pivots))
             for m in range(l):
-                low[m] = jnp.where(here, c[m], low[m])
-            factor = jnp.where(here, -1.0, c[l])
+                low[m] = jnp.where(at0, r[m], jnp.where(at1, s[m] - ratio * r[m], low[m]))
+            low[l] = jnp.where(at1, -ratio, low[l])
+            u = jnp.where(at0, -t, jnp.where(at1, q, t * c[l] - q * c[l + 1]))
+            v = jnp.where(at0, q, jnp.where(at1, -p, p * c[l + 1] - q * c[l]))
             for m in range(8):
-                if m != l:
-                    c[m] = jnp.where(here, 0.0, c[m]) - (factor * r[m]) * inverse
-            c[l] = -(factor * inverse)
+                if m not in (l, l + 1):
+                    c[m] = jnp.where(at0 | at1, 0.0, c[m]) - (r[m] * u + s[m] * v) * inverse
+            c[l], c[l + 1] = -(u * inverse), -(v * inverse)
         t = tree([low[m] * e_row[m] for m in range(8)])
         out.append(lax.rsqrt(pivots) * jnp.where(lane < o + 8, t, 0.0))
         if g == 15:
@@ -90,31 +95,41 @@
     return jnp.concatenate(out, axis=0)
 
 
-def factor_step(k, gram, inv):
-    o, p = B * k, B * (k + 1)
-    diagonal = inverse_factor(gram[o:p, o:p])
+def factor_step(k, diagonal, gram, inv):
+    o, p, n = B * k, B * (k + 1), B * (k + 2)
+    x = inverse_factor(diagonal)
+    inv[o:p, o:p] = x
+    if k < 3:
+        near = mm6(gram[p:n, o:p], x, NT)
+        diagonal = gram[p:n, p:n] - mm6(near, near, NT)
     if k > 0:
-        inv[o:p, 0:o] = mm6(diagonal, inv[o:p, 0:o], NN)
-    inv[o:p, o:p] = diagonal
+        inv[o:p, 0:o] = mm6(x, inv[o:p, 0:o], NN)
     if k < 3:
-        low = mm6(gram[p:, o:p], diagonal, NT)
-        gram[p:, p:] = gram[p:, p:] - mm6(low, low, NT)
+        low = near
+        if k < 2:
+            far = mm6(gram[n:, o:p], x, NT)
+            gram[n:, p:n] = gram[n:, p:n] - mm6(far, near, NT)
+            gram[n:, n:] = gram[n:, n:] - mm6(far, far, NT)
+            low = jnp.concatenate([near, far], axis=0)
         inv[p:, 0:p] = inv[p:, 0:p] - mm6(low, inv[o:p, 0:p], NN)
+    return diagonal
 
 
 PACKED = [(0, 0), (1, 0), (1, 1), (2, 0), (2, 1), (2, 2), (3, 0), (3, 1), (3, 2), (3, 3)]
 LANES = [(256 * j, min(256, C - 256 * j)) for j in range(7)]
-N_MSG = 78
+N_MSG = 87
 
 
 def sum_kernel(
     mom_hbm, grad_hbm, q_ref,
-    orth_hbm, r_hi_hbm, r_lo_hbm, right_hbm, scale_ref,
+    orth_hbm, r_hi_hbm, r_lo_hbm, scale_ref,
     mom, grad, hi, lo, part, recv1, mid, recv2, p_buf, pt_hi, pt_lo,
-    packed, g_recv0, g_recv1, g_sum, gram, inv, wt, w_recv0, w_recv1, w_sum,
-    orth, r_hi, r_lo, right, col, col_recv,
+    packed, g_recv0, g_recv1, g_sum, gram, inv, w_recv0, w_recv1,
+    orth, col, col_recv,
     load_sem, save_sem, send_sem, recv_sem,
 ):
+    wt, w_sum = mom.at[0:RANK], mom.at[RANK:R]
+    r_hi, r_lo = grad.at[0:RANK], grad.at[RANK:R]
     row, column = lax.axis_index("rows"), lax.axis_index("cols")
     x, core = row // 2, row % 2
     y, z = column // 4, column % 4
@@ -145,10 +160,13 @@
         loads.append(pair)
 
     barrier = pltpu.get_barrier_semaphore()
-    peers = [f(d) for f in (at_x, at_y, at_z) for d in (1, 2, 3)] + [other_core]
+
+    def at_plane(d):
+        return (row, (column + d) % 16)
+
+    peers = [at_x(d) for d in (1, 2, 3)] + [at_plane(d) for d in range(1, 16)] + [other_core]
     for peer in peers:
         pl.semaphore_signal(barrier, inc=1, device_id=peer, device_id_type=MESH)
-    pl.semaphore_wait(barrier, len(peers))
 
     started = []
 
@@ -225,20 +243,21 @@
             lo[rows, :] = rest
 
         product_p(0, i)
+    pl.semaphore_wait(barrier, len(peers))
     p1_0 = scatter_first(0)
     for i in range(4):
         product_p(1, i)
-    p1_1 = scatter_first(1)
     finish(p1_0)
     p2_0 = scatter_second(0)
+    p1_1 = scatter_first(1)
+    finish(p2_0)
+    p3_0 = gather_second(0)
     finish(p1_1)
     p2_1 = scatter_second(1)
-    finish(p2_0)
-    p3_0 = gather_second(0)
+    finish(p3_0)
+    p4_0 = gather_first(0)
     finish(p2_1)
     p3_1 = gather_second(1)
-    finish(p3_0)
-    p4_0 = gather_first(0)
     finish(p3_1)
     p4_1 = gather_first(1)
 
@@ -328,22 +347,26 @@
     g3 = [send(g_sum.at[g_ours], g_sum.at[g_ours], other_core)]
     inv[...] = jnp.zeros((RANK, RANK), f32)
     finish(g3)
+    on = lax.broadcasted_iota(jnp.int32, (B, B), 0) == lax.broadcasted_iota(jnp.int32, (B, B), 1)
+    diagonals = [jnp.where(on, g_sum[B * n : B * n + B, :], 0.0) for n in (0, 2, 5, 9)]
+    down = [lax.rsqrt(jnp.sum(t, axis=1, keepdims=True)) for t in diagonals]
+    across = [lax.rsqrt(jnp.sum(t, axis=0, keepdims=True)) for t in diagonals]
     for n, (i, j) in enumerate(PACKED):
-        gram[B * i : B * i + B, B * j : B * j + B] = g_sum[B * n : B * n + B, :]
-
-    factor_step(0, gram, inv)
+        gram[B * i : B * i + B, B * j : B * j + B] = g_sum[B * n : B * n + B, :] * down[i] * across[j]
+
+    diagonal = factor_step(0, gram[0:B, 0:B], gram, inv)
     finish(w1_1)
     w2_1 = w_gather(1)
-    factor_step(1, gram, inv)
-    factor_step(2, gram, inv)
+    diagonal = factor_step(1, diagonal, gram, inv)
     finish(w2_0)
     w3_0 = w_back(0)
-    factor_step(3, gram, inv)
+    diagonal = factor_step(2, diagonal, gram, inv)
+    factor_step(3, diagonal, gram, inv)
     finish(w2_1)
     w3_1 = w_back(1)
+    inv_hi, inv_lo = split(inv[...] * jnp.concatenate(across, axis=1))
     finish(w3_0 + w3_1)
 
-    inv_hi, inv_lo = split(inv[...])
     squares = jnp.zeros((RANK, B), f32)
     for start, size in LANES:
         lanes = slice(start, start + size)
@@ -351,7 +374,6 @@
         top = mm3((inv_hi[:256, :256], inv_lo[:256, :256]), (w[0][:256], w[1][:256]), NN)
         bottom = mm3((inv_hi[256:], inv_lo[256:]), w, NN)
         r = jnp.concatenate([top, bottom], axis=0)
-        mom[0:RANK, lanes] = r
         r_hi[:, lanes], r_lo[:, lanes] = split(r)
         for i in range(0, size, B):
             squares = squares + r[:, i : i + B] * r[:, i : i + B]
@@ -364,22 +386,15 @@
 
     save(r_hi, r_hi_hbm)
     save(r_lo, r_lo_hbm)
-    col[0] = mm6(jnp.ones((8, B), f32), squares, NT)
-    s1 = [send(col.at[0], col_recv.at[0, d - 1], at_y(d)) for d in (2, 1, 3)]
+    col[...] = mm6(jnp.ones((8, B), f32), squares, NT)
+    exchange = [send(col, col_recv.at[d - 1], at_plane(d)) for d in range(1, 16)]
     for i in range(4):
         rows = slice(256 * i, 256 * i + 256)
         p = split(jnp.concatenate([p_buf[k, rows, :] for k in range(4)], axis=1))
         orth[rows, :] = mm3(p, (inv_hi, inv_lo), NT)
     save(orth, orth_hbm)
-    finish(s1)
-    col[1] = (col[0] + col_recv[0, 0]) + (col_recv[0, 1] + col_recv[0, 2])
-    s2 = [send(col.at[1], col_recv.at[1, d - 1], at_z(d)) for d in (2, 1, 3)]
-    for j in range(13):
-        lanes = slice(B * j, B * j + B)
-        right[lanes, :] = mom[0:RANK, lanes].T
-    save(right, right_hbm)
-    finish(s2)
-    total = (col[1] + col_recv[1, 0]) + (col_recv[1, 1] + col_recv[1, 2])
+    finish(exchange)
+    total = tree([col[...]] + [col_recv[d] for d in range(15)])
     scale_ref[...] = lax.rsqrt(total * (1.0 / COLS) + epsilon)
     for copy in saves:
         copy.wait()
@@ -396,11 +411,10 @@
             jax.ShapeDtypeStruct((R, RANK), f32),
             jax.ShapeDtypeStruct((RANK, C), bf16),
             jax.ShapeDtypeStruct((RANK, C), bf16),
-            jax.ShapeDtypeStruct((C, RANK), f32),
             jax.ShapeDtypeStruct((8, RANK), f32),
         ],
         in_specs=[hbm, hbm, vmem],
-        out_specs=[hbm] * 4 + [vmem],
+        out_specs=[hbm] * 3 + [vmem],
         scratch_shapes=[
             pltpu.VMEM((R, C), f32),
             pltpu.VMEM((R, C), bf16),
@@ -419,31 +433,38 @@
             pltpu.VMEM((1280, B), f32),
             pltpu.VMEM((RANK, RANK), f32),
             pltpu.VMEM((RANK, RANK), f32),
-            pltpu.VMEM((RANK, C), f32),
             pltpu.VMEM((2, B, C), f32),
             pltpu.VMEM((2, 3, 32, C), f32),
-            pltpu.VMEM((RANK, C), f32),
             pltpu.VMEM((R, RANK), f32),
-            pltpu.VMEM((RANK, C), bf16),
-            pltpu.VMEM((RANK, C), bf16),
-            pltpu.VMEM((C, RANK), f32),
-            pltpu.VMEM((2, 8, RANK), f32),
-            pltpu.VMEM((2, 3, 8, RANK), f32),
+            pltpu.VMEM((8, RANK), f32),
+            pltpu.VMEM((15, 8, RANK), f32),
             pltpu.SemaphoreType.DMA((8,)),
-            pltpu.SemaphoreType.DMA((4,)),
+            pltpu.SemaphoreType.DMA((3,)),
             pltpu.SemaphoreType.DMA((N_MSG,)),
             pltpu.SemaphoreType.DMA((N_MSG,)),
         ],
         compiler_params=pltpu.CompilerParams(
-            collective_id=0, has_side_effects=True, vmem_limit_bytes=60 << 20
+            collective_id=0, has_side_effects=True, vmem_limit_bytes=44 << 20
         ),
         name="sums",
     )(momentum, grad, q_basis)
 
 
-def output_kernel(mom, grad, orth_ref, r_hi, r_lo, right, scale_ref, mom_out, q_out, update_out):
+STEPS = 4
+Q_CHUNKS = [range(13 * i // STEPS, 13 * (i + 1) // STEPS) for i in range(STEPS)]
+
+
+def output_kernel(mom, grad, orth_ref, r_hi, r_lo, scale_ref, mom_out, q_out, update_out):
     scale = scale_ref[0:1, :]
-    q_out[...] = (right[...] * scale).astype(bf16)
+    for i, chunks in enumerate(Q_CHUNKS):
+
+        @pl.when(pl.program_id(0) == i)
+        def _(chunks=chunks):
+            for j in chunks:
+                lanes = slice(B * j, B * j + B)
+                r = r_hi[:, lanes].astype(f32) + r_lo[:, lanes].astype(f32)
+                q_out[lanes, :] = (r.T * scale).astype(bf16)
+
     orth = orth_ref[...]
     scaled = split(orth * (scale * (float(ROWS) / RANK) ** 0.5))
     step = (orth * feedback_rate).astype(bf16)
@@ -455,26 +476,22 @@
         update_out[:, lanes] = mm3(scaled, (top, r_lo[:, lanes]), NN).astype(bf16)
 
 
-def outputs(momentum, grad, orth, r_hi, r_lo, right, scale):
-    steps = 4
-    rows = R // steps
+def outputs(momentum, grad, orth, r_hi, r_lo, scale):
     whole = lambda *shape: pl.BlockSpec(shape, lambda i: (0,) * len(shape))
-    slab = lambda n, width: pl.BlockSpec((n // steps, width), lambda i: (i, 0))
+    slab = lambda width: pl.BlockSpec((R // STEPS, width), lambda i: (i, 0))
     return pl.pallas_call(
         output_kernel,
-        grid=(steps,),
+        grid=(STEPS,),
         out_shape=[
             jax.ShapeDtypeStruct((R, C), f32),
             jax.ShapeDtypeStruct((C, RANK), bf16),
             jax.ShapeDtypeStruct((R, C), bf16),
         ],
-        in_specs=[
-            slab(R, C), slab(R, C), slab(R, RANK), whole(RANK, C), whole(RANK, C), slab(C, RANK), whole(8, RANK),
-        ],
-        out_specs=[slab(R, C), slab(C, RANK), slab(R, C)],
-        compiler_params=pltpu.CompilerParams(vmem_limit_bytes=60 << 20),
+        in_specs=[slab(C), slab(C), slab(RANK), whole(RANK, C), whole(RANK, C), whole(8, RANK)],
+        out_specs=[slab(C), whole(C, RANK), slab(C)],
+        compiler_params=pltpu.CompilerParams(vmem_limit_bytes=36 << 20),
         name="outputs",
-    )(momentum, grad, orth, r_hi, r_lo, right, scale)
+    )(momentum, grad, orth, r_hi, r_lo, scale)
 
 
 def body(momentum, grad, q_basis):

time: 128 us -> 122 us (0.953)
  Pallas kernels: 127 us -> 119 us
  local copies, waits for them, and re-layouts: 0 us -> 1.45 us
    pallas_call x1, Pallas kernels: 113 us -> 108 us  [sums(): pl.pallas_call(sum_kernel, out_shape=[jax.ShapeDtypeStruct((R, RANK), f32...]
    pallas_call x1, Pallas kernels: 14.2 us -> 10.9 us  [outputs(): pl.pallas_call(output_kernel, grid=(STEPS,), out_shape=[jax.ShapeDtypeStr...]
    unnamed x0 -> x6, local copies, waits for them, and re-layouts: none -> 1.45 us
where the time goes in v3:
time: 122 us; the launch traced here: 121 us
  Pallas kernels  119 us (98%)
  local copies, waits for them, and re-layouts  1.45 us (1%)
    pallas_call x1, Pallas kernels, sums(): pl.pallas_call(sum_kernel, out_shape=[jax.ShapeDtypeStruct((R, RANK), f32...  108 us
    pallas_call x1, Pallas kernels, outputs(): pl.pallas_call(output_kernel, grid=(STEPS,), out_shape=[jax.ShapeDtypeStr...  10.9 us

profile of v3, /device:TPU:0, one launch (start us, length us, event | category | flops | bytes accessed | tf_op | source)
XLA Modules:
  0.0 121.1 jit_solution(16432334578479934945)
XLA Ops:
  0.6 0.0 copy-start.2
  0.6 1.4 %copy-done.2 = bf16[1664,512]{1,0:T(8,128)(2,1)S(1)} copy-done((bf16[1664,512]{1,0:T(8,128)(2,1)S(1)}, bf16[1664,512]{1,0:T(8,128)(2,1)}, u32[]{:S(2)}) %copy-start.2) | copy-done | bytes 1703960
  2.1 0.0 copy-start
  2.1 0.0 copy-start.1
  2.1 108.1 %sums.1 = (f32[1024,512]{1,0:T(8,128)S(1)}, bf16[512,1664]{1,0:T(8,128)(2,1)S(1)}, bf16[512,1664]{1,0:T(8,128)(2,1)S(1)}, f32[8,512]{1,0:T(8,128)S(1)}) custom-call(f32[1024,1664]{1,0:T(8,128)} %mom.1, bf16[1024,1664]{1,0:T(8,128)(2,1)} %grad.1, bf16[1664,512]{1,0:T(8,128)(2,1)S(1)} %copy-done.2), custom_call_target="tpu_custom_call" | custom-call | tf_op jit(solution)/shard_map/sums/pallas_call | solution.py:408
  110.2 0.0 copy-done
  110.2 0.0 copy-done.1
  110.2 10.9 %outputs.1 = (f32[1024,1664]{1,0:T(8,128)}, bf16[1664,512]{1,0:T(8,128)(2,1)}, bf16[1024,1664]{1,0:T(8,128)(2,1)}) custom-call(f32[1024,1664]{1,0:T(8,128)S(1)} %copy-done, bf16[1024,1664]{1,0:T(8,128)(2,1)S(1)} %copy-done.1, f32[1024,512]{1,0:T(8,128)S(1)} %get-tuple-element.7.orth_ref, bf16[512,1664]{1,0:T(8,128)(2,1)S(1)} %get-tuple-element.8.r_hi, ...), custom_call_target="tpu_custom_call" | custom-call | tf_op jit(solution)/shard_map/outputs/pallas_call | solution.py:482
Async XLA Ops:
  0.6 1.5 %copy-start.2 = (bf16[1664,512]{1,0:T(8,128)(2,1)S(1)}, bf16[1664,512]{1,0:T(8,128)(2,1)}, u32[]{:S(2)}) copy-start(bf16[1664,512]{1,0:T(8,128)(2,1)} %q_ref.1) | copy-start | bytes 5111812
  2.1 108.1 %copy-start = (f32[1024,1664]{1,0:T(8,128)S(1)}, f32[1024,1664]{1,0:T(8,128)}, u32[]{:S(2)}) copy-start(f32[1024,1664]{1,0:T(8,128)} %mom.1) | copy-start | bytes 20447236
  2.1 108.1 %copy-start.1 = (bf16[1024,1664]{1,0:T(8,128)(2,1)S(1)}, bf16[1024,1664]{1,0:T(8,128)(2,1)}, u32[]{:S(2)}) copy-start(bf16[1024,1664]{1,0:T(8,128)(2,1)} %grad.1) | copy-start | bytes 10223620

commit v4 on v3

--- a/solution.py
+++ b/solution.py
@@ -117,14 +117,14 @@
 
 PACKED = [(0, 0), (1, 0), (1, 1), (2, 0), (2, 1), (2, 2), (3, 0), (3, 1), (3, 2), (3, 3)]
 LANES = [(256 * j, min(256, C - 256 * j)) for j in range(7)]
-N_MSG = 87
+N_MSG = 91
 
 
 def sum_kernel(
-    mom_hbm, grad_hbm, q_ref,
+    mom_hbm, grad_hbm, q_hbm,
     orth_hbm, r_hi_hbm, r_lo_hbm, scale_ref,
-    mom, grad, hi, lo, part, recv1, mid, recv2, p_buf, pt_hi, pt_lo,
-    packed, g_recv0, g_recv1, g_sum, gram, inv, w_recv0, w_recv1,
+    mom, grad, q_ref, hi, lo, part, recv1, mid, recv2, p_buf, pt_hi, pt_lo,
+    packed, g_recv0, g_recv1, g_sum, gram, inv, w_recv0, w_recv1, w_recv2,
     orth, col, col_recv,
     load_sem, save_sem, send_sem, recv_sem,
 ):
@@ -158,6 +158,9 @@
         for copy in pair:
             copy.start()
         loads.append(pair)
+        if i == 0:
+            load_q = pltpu.make_async_copy(q_hbm, q_ref, load_sem.at[8])
+            load_q.start()
 
     barrier = pltpu.get_barrier_semaphore()
 
@@ -242,6 +245,8 @@
             hi[rows, :] = top
             lo[rows, :] = rest
 
+        if i == 0:
+            load_q.wait()
         product_p(0, i)
     pl.semaphore_wait(barrier, len(peers))
     p1_0 = scatter_first(0)
@@ -295,20 +300,54 @@
     def theirs(s):
         return block(256 * s + B * (1 - core), B)
 
-    def slab(s, i):
-        return block(256 * s + B * core + 32 * i, 32)
+    pair_a, pair_b = x + 1 - 2 * (x % 2), 3 - x
+    group = (x // 2, ((x + 1) // 2) % 2)
+    place = (x % 2, x // 2)
+    halves = (slice(0, 896), slice(896, 1664))
+
+    def along_x(other):
+        return (other * 2 + core, column)
+
+    far = (along_x(pair_b), along_x(pair_a))
+    near = (along_x(pair_a), along_x(pair_b))
+
+    def group_rows(s, g):
+        return block(256 * s + B * core + 64 * g, 64)
+
+    def slab(s, h, i):
+        return block(256 * s + B * core + 64 * group[h] + 32 * i, 32)
 
     def w_cores(s):
         return [send(wt.at[theirs(s)], w_recv0.at[s], other_core)]
 
-    def w_scatter(s):
+    def w_scatter_far(s):
         wt[ours(s), :] = wt[ours(s), :] + w_recv0[s]
-        return [send(wt.at[slab(s, (x + d) % 4)], w_recv1.at[s, d - 1], at_x(d)) for d in (2, 1, 3)]
-
-    def w_gather(s):
-        mine = slab(s, x)
-        w_sum[mine, :] = (wt[mine, :] + w_recv1[s, 0]) + (w_recv1[s, 1] + w_recv1[s, 2])
-        return [send(w_sum.at[mine], w_sum.at[mine], at_x(d)) for d in (2, 1, 3)]
+        return [
+            send(wt.at[group_rows(s, 1 - group[h]), halves[h]], w_recv1.at[s, :, halves[h]], far[h]) for h in range(2)
+        ]
+
+    def w_scatter_near(s):
+        copies = []
+        for h in range(2):
+            rows = group_rows(s, group[h])
+            wt[rows, halves[h]] = wt[rows, halves[h]] + w_recv1[s, :, halves[h]]
+            copies.append(send(wt.at[slab(s, h, 1 - place[h]), halves[h]], w_recv2.at[s, :, halves[h]], near[h]))
+        return copies
+
+    def w_gather_near(s):
+        copies = []
+        for h in range(2):
+            mine = slab(s, h, place[h])
+            w_sum[mine, halves[h]] = wt[mine, halves[h]] + w_recv2[s, :, halves[h]]
+            copies.append(send(w_sum.at[mine, halves[h]], w_sum.at[mine, halves[h]], near[h]))
+        return copies
+
+    def w_gather_far(s):
+        copies = []
+        for h in range(2):
+            rows = group_rows(s, group[h])
+            copies.append(send(w_sum.at[rows, halves[h]], w_sum.at[rows, halves[h]], far[h]))
+        return copies
 
     def w_back(s):
         return [send(w_sum.at[ours(s)], w_sum.at[ours(s)], other_core)]
@@ -319,33 +358,37 @@
     w0_0 = w_cores(0)
     gram_block(0, 0)
     finish(w0_0)
-    w1_0 = w_scatter(0)
+    w1_0 = w_scatter_far(0)
     finish(p4_1)
     transpose_p(1)
     gram_block(1, 0)
     gram_block(1, 1)
     g_ours, g_theirs = block(640 * core, 640), block(640 * (1 - core), 640)
     g0 = [send(packed.at[g_theirs], g_recv0, other_core)]
+    finish(w1_0)
+    w2_0 = w_scatter_near(0)
+    finish(g0)
+    packed[g_ours, :] = packed[g_ours, :] + g_recv0[...]
+
+    def g_slab(i):
+        return block(640 * core + 160 * i, 160)
+
+    g1 = [send(packed.at[g_slab((x + d) % 4)], g_recv1.at[d - 1], at_x(d)) for d in (2, 1, 3)]
     product_w(1)
     w0_1 = w_cores(1)
-    finish(g0)
-    packed[g_ours, :] = packed[g_ours, :] + g_recv0[...]
-
-    def g_slab(i):
-        return block(640 * core + 160 * i, 160)
-
-    g1 = [send(packed.at[g_slab((x + d) % 4)], g_recv1.at[d - 1], at_x(d)) for d in (2, 1, 3)]
-    finish(w0_1)
     finish(g1)
     g_mine = g_slab(x)
     g_sum[g_mine, :] = (packed[g_mine, :] + g_recv1[0]) + (g_recv1[1] + g_recv1[2])
     g2 = [send(g_sum.at[g_mine], g_sum.at[g_mine], at_x(d)) for d in (2, 1, 3)]
-    w1_1 = w_scatter(1)
-    finish(w1_0)
-    w2_0 = w_gather(0)
+    finish(w2_0)
+    w3_0 = w_gather_near(0)
+    finish(w0_1)
+    w1_1 = w_scatter_far(1)
     finish(g2)
     g3 = [send(g_sum.at[g_ours], g_sum.at[g_ours], other_core)]
     inv[...] = jnp.zeros((RANK, RANK), f32)
+    finish(w3_0)
+    w4_0 = w_gather_far(0)
     finish(g3)
     on = lax.broadcasted_iota(jnp.int32, (B, B), 0) == lax.broadcasted_iota(jnp.int32, (B, B), 1)
     diagonals = [jnp.where(on, g_sum[B * n : B * n + B, :], 0.0) for n in (0, 2, 5, 9)]
@@ -356,27 +399,34 @@
 
     diagonal = factor_step(0, gram[0:B, 0:B], gram, inv)
     finish(w1_1)
-    w2_1 = w_gather(1)
+    w2_1 = w_scatter_near(1)
     diagonal = factor_step(1, diagonal, gram, inv)
-    finish(w2_0)
-    w3_0 = w_back(0)
+    finish(w2_1)
+    w3_1 = w_gather_near(1)
+    finish(w4_0)
+    w5_0 = w_back(0)
     diagonal = factor_step(2, diagonal, gram, inv)
+    finish(w3_1)
+    w4_1 = w_gather_far(1)
     factor_step(3, diagonal, gram, inv)
-    finish(w2_1)
-    w3_1 = w_back(1)
+    finish(w4_1)
+    w5_1 = w_back(1)
     inv_hi, inv_lo = split(inv[...] * jnp.concatenate(across, axis=1))
-    finish(w3_0 + w3_1)
-
-    squares = jnp.zeros((RANK, B), f32)
-    for start, size in LANES:
-        lanes = slice(start, start + size)
-        w = split(w_sum[:, lanes])
-        top = mm3((inv_hi[:256, :256], inv_lo[:256, :256]), (w[0][:256], w[1][:256]), NN)
-        bottom = mm3((inv_hi[256:], inv_lo[256:]), w, NN)
-        r = jnp.concatenate([top, bottom], axis=0)
-        r_hi[:, lanes], r_lo[:, lanes] = split(r)
-        for i in range(0, size, B):
-            squares = squares + r[:, i : i + B] * r[:, i : i + B]
+
+    def right_half(rows, depth):
+        squares = jnp.zeros((256, B), f32)
+        for start, size in LANES:
+            lanes = slice(start, start + size)
+            r = mm3((inv_hi[rows, :depth], inv_lo[rows, :depth]), split(w_sum[:depth, lanes]), NN)
+            r_hi[rows, lanes], r_lo[rows, lanes] = split(r)
+            for i in range(0, size, B):
+                squares = squares + r[:, i : i + B] * r[:, i : i + B]
+        return squares
+
+    finish(w5_0)
+    upper = right_half(slice(0, 256), 256)
+    finish(w5_1)
+    squares = jnp.concatenate([upper, right_half(slice(256, 512), 512)], axis=0)
     saves = []
 
     def save(src, dst):
@@ -413,11 +463,12 @@
             jax.ShapeDtypeStruct((RANK, C), bf16),
             jax.ShapeDtypeStruct((8, RANK), f32),
         ],
-        in_specs=[hbm, hbm, vmem],
+        in_specs=[hbm] * 3,
         out_specs=[hbm] * 3 + [vmem],
         scratch_shapes=[
             pltpu.VMEM((R, C), f32),
             pltpu.VMEM((R, C), bf16),
+            pltpu.VMEM((C, RANK), bf16),
             pltpu.VMEM((R, C), bf16),
             pltpu.VMEM((R, C), bf16),
             pltpu.VMEM((4, R, B), f32),
@@ -434,11 +485,12 @@
             pltpu.VMEM((RANK, RANK), f32),
             pltpu.VMEM((RANK, RANK), f32),
             pltpu.VMEM((2, B, C), f32),
-            pltpu.VMEM((2, 3, 32, C), f32),
+            pltpu.VMEM((2, 64, C), f32),
+            pltpu.VMEM((2, 32, C), f32),
             pltpu.VMEM((R, RANK), f32),
             pltpu.VMEM((8, RANK), f32),
             pltpu.VMEM((15, 8, RANK), f32),
-            pltpu.SemaphoreType.DMA((8,)),
+            pltpu.SemaphoreType.DMA((9,)),
             pltpu.SemaphoreType.DMA((3,)),
             pltpu.SemaphoreType.DMA((N_MSG,)),
             pltpu.SemaphoreType.DMA((N_MSG,)),

time: 122 us -> 126 us (1.033)
  Pallas kernels: 119 us -> 122 us
    pallas_call x1, Pallas kernels: 108 us -> 111 us  [sums(): pl.pallas_call(sum_kernel, out_shape=[jax.ShapeDtypeStruct((R, RANK), f32...]
where the time goes in v4:
time: 126 us; the launch traced here: 124 us
  Pallas kernels  122 us (97%)
  local copies, waits for them, and re-layouts  1.45 us (1%)
    pallas_call x1, Pallas kernels, sums(): pl.pallas_call(sum_kernel, out_shape=[jax.ShapeDtypeStruct((R, RANK), f32...  111 us
    pallas_call x1, Pallas kernels, outputs(): pl.pallas_call(output_kernel, grid=(STEPS,), out_shape=[jax.ShapeDtypeStr...  10.9 us

profile of v4, /device:TPU:0, one launch (start us, length us, event | category | flops | bytes accessed | tf_op | source)
XLA Modules:
  0.0 124.2 jit_solution(14386919694086875413)
XLA Ops:
  0.6 0.0 copy-start.2
  0.6 1.4 %copy-done.2 = bf16[1664,512]{1,0:T(8,128)(2,1)S(1)} copy-done((bf16[1664,512]{1,0:T(8,128)(2,1)S(1)}, bf16[1664,512]{1,0:T(8,128)(2,1)}, u32[]{:S(2)}) %copy-start.2) | copy-done | bytes 1703960
  2.1 0.0 copy-start
  2.1 0.0 copy-start.1
  2.1 111.2 %sums.1 = (f32[1024,512]{1,0:T(8,128)S(1)}, bf16[512,1664]{1,0:T(8,128)(2,1)S(1)}, bf16[512,1664]{1,0:T(8,128)(2,1)S(1)}, f32[8,512]{1,0:T(8,128)S(1)}) custom-call(f32[1024,1664]{1,0:T(8,128)} %mom.1, bf16[1024,1664]{1,0:T(8,128)(2,1)} %grad.1, bf16[1664,512]{1,0:T(8,128)(2,1)S(1)} %copy-done.2), custom_call_target="tpu_custom_call" | custom-call | tf_op jit(solution)/shard_map/sums/pallas_call | solution.py:458
  113.3 0.0 copy-done
  113.3 0.0 copy-done.1
  113.3 10.9 %outputs.1 = (f32[1024,1664]{1,0:T(8,128)}, bf16[1664,512]{1,0:T(8,128)(2,1)}, bf16[1024,1664]{1,0:T(8,128)(2,1)}) custom-call(f32[1024,1664]{1,0:T(8,128)S(1)} %copy-done, bf16[1024,1664]{1,0:T(8,128)(2,1)S(1)} %copy-done.1, f32[1024,512]{1,0:T(8,128)S(1)} %get-tuple-element.7.orth_ref, bf16[512,1664]{1,0:T(8,128)(2,1)S(1)} %get-tuple-element.8.r_hi, ...), custom_call_target="tpu_custom_call" | custom-call | tf_op jit(solution)/shard_map/outputs/pallas_call | solution.py:534
Async XLA Ops:
  0.6 1.5 %copy-start.2 = (bf16[1664,512]{1,0:T(8,128)(2,1)S(1)}, bf16[1664,512]{1,0:T(8,128)(2,1)}, u32[]{:S(2)}) copy-start(bf16[1664,512]{1,0:T(8,128)(2,1)} %q_hbm.1) | copy-start | bytes 5111812
  2.1 111.2 %copy-start = (f32[1024,1664]{1,0:T(8,128)S(1)}, f32[1024,1664]{1,0:T(8,128)}, u32[]{:S(2)}) copy-start(f32[1024,1664]{1,0:T(8,128)} %mom.1) | copy-start | bytes 20447236
  2.1 111.2 %copy-start.1 = (bf16[1024,1664]{1,0:T(8,128)(2,1)S(1)}, bf16[1024,1664]{1,0:T(8,128)(2,1)}, u32[]{:S(2)}) copy-start(bf16[1024,1664]{1,0:T(8,128)(2,1)} %grad.1) | copy-start | bytes 10223620

commit v5 on v4

--- a/solution.py
+++ b/solution.py
@@ -117,7 +117,7 @@
 
 PACKED = [(0, 0), (1, 0), (1, 1), (2, 0), (2, 1), (2, 2), (3, 0), (3, 1), (3, 2), (3, 3)]
 LANES = [(256 * j, min(256, C - 256 * j)) for j in range(7)]
-N_MSG = 91
+N_MSG = 159
 
 
 def sum_kernel(
@@ -189,49 +189,48 @@
 
     at_first, at_second = (at_y, at_z), (at_z, at_y)
     first, second = (y, z), (z, y)
-    groups = lambda s: [(2 * s + h, h) for h in range(2)]
-
-    def product_p(s, i):
+
+    def product_p(pair, i):
         rows = pl.ds(256 * i, 256)
-        q = q_ref[:, 256 * s : 256 * s + 256]
+        q = q_ref[:, 256 * pair : 256 * pair + 256]
         value = mm(hi[rows, :], q, NN) + mm(lo[rows, :], q, NN)
-        part[2 * s, rows, :] = value[:, :B]
-        part[2 * s + 1, rows, :] = value[:, B:]
+        part[2 * pair, rows, :] = value[:, :B]
+        part[2 * pair + 1, rows, :] = value[:, B:]
 
     def scatter_first(s):
         copies = []
         for d in (2, 1, 3):
-            for k, h in groups(s):
-                rows = block(((first[h] + d) % 4) * 256, 256)
-                copies.append(send(part.at[k, rows], recv1.at[k, d - 1], at_first[h](d)))
+            for h in range(2):
+                rows = block(512 * h + ((first[h] + d) % 4) * 128, 128)
+                copies.append(send(part.at[s, rows], recv1.at[s, h, d - 1], at_first[h](d)))
         return copies
 
     def scatter_second(s):
         copies = []
-        for k, h in groups(s):
-            rows = block(first[h] * 256, 256)
-            mid[k] = (part[k, rows, :] + recv1[k, 0]) + (recv1[k, 1] + recv1[k, 2])
+        for h in range(2):
+            rows = block(512 * h + first[h] * 128, 128)
+            mid[s, h] = (part[s, rows, :] + recv1[s, h, 0]) + (recv1[s, h, 1] + recv1[s, h, 2])
             for d in (2, 1, 3):
-                rows = block(((second[h] + d) % 4) * 64, 64)
-                copies.append(send(mid.at[k, rows], recv2.at[k, d - 1], at_second[h](d)))
+                rows = block(((second[h] + d) % 4) * 32, 32)
+                copies.append(send(mid.at[s, h, rows], recv2.at[s, h, d - 1], at_second[h](d)))
         return copies
 
     def gather_second(s):
         copies = []
-        for k, h in groups(s):
-            rows = block(second[h] * 64, 64)
-            mine = block(first[h] * 256 + second[h] * 64, 64)
-            p_buf[k, mine, :] = (mid[k, rows, :] + recv2[k, 0]) + (recv2[k, 1] + recv2[k, 2])
+        for h in range(2):
+            rows = block(second[h] * 32, 32)
+            mine = block(512 * h + first[h] * 128 + second[h] * 32, 32)
+            p_buf[s, mine, :] = (mid[s, h, rows, :] + recv2[s, h, 0]) + (recv2[s, h, 1] + recv2[s, h, 2])
             for d in (2, 1, 3):
-                copies.append(send(p_buf.at[k, mine], p_buf.at[k, mine], at_second[h](d)))
+                copies.append(send(p_buf.at[s, mine], p_buf.at[s, mine], at_second[h](d)))
         return copies
 
     def gather_first(s):
         copies = []
-        for k, h in groups(s):
-            mine = block(first[h] * 256, 256)
+        for h in range(2):
+            mine = block(512 * h + first[h] * 128, 128)
             for d in (2, 1, 3):
-                copies.append(send(p_buf.at[k, mine], p_buf.at[k, mine], at_first[h](d)))
+                copies.append(send(p_buf.at[s, mine], p_buf.at[s, mine], at_first[h](d)))
         return copies
 
     for i in range(4):
@@ -249,30 +248,10 @@
             load_q.wait()
         product_p(0, i)
     pl.semaphore_wait(barrier, len(peers))
-    p1_0 = scatter_first(0)
-    for i in range(4):
-        product_p(1, i)
-    finish(p1_0)
-    p2_0 = scatter_second(0)
-    p1_1 = scatter_first(1)
-    finish(p2_0)
-    p3_0 = gather_second(0)
-    finish(p1_1)
-    p2_1 = scatter_second(1)
-    finish(p3_0)
-    p4_0 = gather_first(0)
-    finish(p2_1)
-    p3_1 = gather_second(1)
-    finish(p3_1)
-    p4_1 = gather_first(1)
-
     def transpose_p(s):
-        for k, _ in groups(s):
-            for i in range(4):
-                rows = slice(256 * i, 256 * i + 256)
-                top, rest = split(p_buf[k, rows, :].T)
-                pt_hi[B * k : B * k + B, rows] = top
-                pt_lo[B * k : B * k + B, rows] = rest
+        for i in range(4):
+            rows = slice(256 * i, 256 * i + 256)
+            pt_hi[B * s : B * s + B, rows], pt_lo[B * s : B * s + B, rows] = split(p_buf[s, rows, :].T)
 
     def gram_block(s, t):
         a, b = slice(256 * s, 256 * s + 256), slice(256 * t, 256 * t + 256)
@@ -283,7 +262,7 @@
                 packed[B * n : B * n + B, :] = value[r : r + B, c : c + B]
 
     def product_w(s):
-        rows = slice(256 * s, 256 * s + 256)
+        rows = slice(B * s, B * s + B)
 
         def chunk(lanes):
             wt[rows, lanes] = mm3((pt_hi[rows, :], pt_lo[rows, :]), (hi[:, lanes], lo[:, lanes]), NN)
@@ -295,10 +274,10 @@
         chunk(slice(1536, 1664))
 
     def ours(s):
-        return block(256 * s + B * core, B)
+        return block(B * s + 64 * core, 64)
 
     def theirs(s):
-        return block(256 * s + B * (1 - core), B)
+        return block(B * s + 64 * (1 - core), 64)
 
     pair_a, pair_b = x + 1 - 2 * (x % 2), 3 - x
     group = (x // 2, ((x + 1) // 2) % 2)
@@ -312,10 +291,10 @@
     near = (along_x(pair_a), along_x(pair_b))
 
     def group_rows(s, g):
-        return block(256 * s + B * core + 64 * g, 64)
+        return block(B * s + 64 * core + 32 * g, 32)
 
     def slab(s, h, i):
-        return block(256 * s + B * core + 64 * group[h] + 32 * i, 32)
+        return block(B * s + 64 * core + 32 * group[h] + 16 * i, 16)
 
     def w_cores(s):
         return [send(wt.at[theirs(s)], w_recv0.at[s], other_core)]
@@ -352,21 +331,81 @@
     def w_back(s):
         return [send(w_sum.at[ours(s)], w_sum.at[ours(s)], other_core)]
 
-    finish(p4_0)
+    p1, p2, p3, p4 = {}, {}, {}, {}
+    p1[0] = scatter_first(0)
+    p1[1] = scatter_first(1)
+    for i in range(4):
+        product_p(1, i)
+    finish(p1[0])
+    p2[0] = scatter_second(0)
+    p1[2] = scatter_first(2)
+    finish(p1[1])
+    p2[1] = scatter_second(1)
+    p1[3] = scatter_first(3)
+    finish(p2[0])
+    p3[0] = gather_second(0)
+    finish(p1[2])
+    p2[2] = scatter_second(2)
+    finish(p2[1])
+    p3[1] = gather_second(1)
+    finish(p3[0])
+    p4[0] = gather_first(0)
+    finish(p1[3])
+    p2[3] = scatter_second(3)
+    finish(p2[2])
+    p3[2] = gather_second(2)
+    finish(p3[1])
+    p4[1] = gather_first(1)
+    finish(p2[3])
+    p3[3] = gather_second(3)
+    finish(p3[2])
+    p4[2] = gather_first(2)
+    w0, w1, w2, w3, w4, w5 = {}, {}, {}, {}, {}, {}
+
+    def start_w(s):
+        product_w(s)
+        w0[s] = w_cores(s)
+
+    def scatter_far(s):
+        finish(w0[s])
+        w1[s] = w_scatter_far(s)
+
+    def scatter_near(s):
+        finish(w1[s])
+        w2[s] = w_scatter_near(s)
+
+    def gather_near(s):
+        finish(w2[s])
+        w3[s] = w_gather_near(s)
+
+    def gather_far(s):
+        finish(w3[s])
+        w4[s] = w_gather_far(s)
+
+    def gather_cores(s):
+        finish(w4[s])
+        w5[s] = w_back(s)
+
+    finish(p4[0])
     transpose_p(0)
-    product_w(0)
-    w0_0 = w_cores(0)
+    start_w(0)
+    finish(p3[3])
+    p4[3] = gather_first(3)
+    finish(p4[1])
+    transpose_p(1)
+    start_w(1)
+    scatter_far(0)
+    scatter_far(1)
     gram_block(0, 0)
-    finish(w0_0)
-    w1_0 = w_scatter_far(0)
-    finish(p4_1)
-    transpose_p(1)
+    finish(p4[2])
+    transpose_p(2)
+    finish(p4[3])
+    transpose_p(3)
     gram_block(1, 0)
     gram_block(1, 1)
     g_ours, g_theirs = block(640 * core, 640), block(640 * (1 - core), 640)
     g0 = [send(packed.at[g_theirs], g_recv0, other_core)]
-    finish(w1_0)
-    w2_0 = w_scatter_near(0)
+    scatter_near(0)
     finish(g0)
     packed[g_ours, :] = packed[g_ours, :] + g_recv0[...]
 
@@ -374,21 +413,20 @@
         return block(640 * core + 160 * i, 160)
 
     g1 = [send(packed.at[g_slab((x + d) % 4)], g_recv1.at[d - 1], at_x(d)) for d in (2, 1, 3)]
-    product_w(1)
-    w0_1 = w_cores(1)
+    scatter_near(1)
+    start_w(2)
+    start_w(3)
+    inv[...] = jnp.zeros((RANK, RANK), f32)
     finish(g1)
     g_mine = g_slab(x)
     g_sum[g_mine, :] = (packed[g_mine, :] + g_recv1[0]) + (g_recv1[1] + g_recv1[2])
     g2 = [send(g_sum.at[g_mine], g_sum.at[g_mine], at_x(d)) for d in (2, 1, 3)]
-    finish(w2_0)
-    w3_0 = w_gather_near(0)
-    finish(w0_1)
-    w1_1 = w_scatter_far(1)
+    gather_near(0)
+    gather_near(1)
     finish(g2)
     g3 = [send(g_sum.at[g_ours], g_sum.at[g_ours], other_core)]
-    inv[...] = jnp.zeros((RANK, RANK), f32)
-    finish(w3_0)
-    w4_0 = w_gather_far(0)
+    scatter_far(2)
+    scatter_far(3)
     finish(g3)
     on = lax.broadcasted_iota(jnp.int32, (B, B), 0) == lax.broadcasted_iota(jnp.int32, (B, B), 1)
     diagonals = [jnp.where(on, g_sum[B * n : B * n + B, :], 0.0) for n in (0, 2, 5, 9)]
@@ -398,35 +436,46 @@
         gram[B * i : B * i + B, B * j : B * j + B] = g_sum[B * n : B * n + B, :] * down[i] * across[j]
 
     diagonal = factor_step(0, gram[0:B, 0:B], gram, inv)
-    finish(w1_1)
-    w2_1 = w_scatter_near(1)
+    scatter_near(2)
+    scatter_near(3)
+    gather_far(0)
+    gather_far(1)
     diagonal = factor_step(1, diagonal, gram, inv)
-    finish(w2_1)
-    w3_1 = w_gather_near(1)
-    finish(w4_0)
-    w5_0 = w_back(0)
+    gather_near(2)
+    gather_near(3)
     diagonal = factor_step(2, diagonal, gram, inv)
-    finish(w3_1)
-    w4_1 = w_gather_far(1)
+    gather_far(2)
+    gather_far(3)
+    gather_cores(0)
+    gather_cores(1)
     factor_step(3, diagonal, gram, inv)
-    finish(w4_1)
-    w5_1 = w_back(1)
+    gather_cores(2)
+    gather_cores(3)
     inv_hi, inv_lo = split(inv[...] * jnp.concatenate(across, axis=1))
 
-    def right_half(rows, depth):
-        squares = jnp.zeros((256, B), f32)
-        for start, size in LANES:
-            lanes = slice(start, start + size)
-            r = mm3((inv_hi[rows, :depth], inv_lo[rows, :depth]), split(w_sum[:depth, lanes]), NN)
-            r_hi[rows, lanes], r_lo[rows, lanes] = split(r)
-            for i in range(0, size, B):
-                squares = squares + r[:, i : i + B] * r[:, i : i + B]
+    finish(w5[0] + w5[1])
+
+    def keep(rows, lanes, r, squares):
+        r_hi[rows, lanes], r_lo[rows, lanes] = split(r)
+        for i in range(0, r.shape[1], B):
+            squares = squares + r[:, i : i + B] * r[:, i : i + B]
         return squares
 
-    finish(w5_0)
-    upper = right_half(slice(0, 256), 256)
-    finish(w5_1)
-    squares = jnp.concatenate([upper, right_half(slice(256, 512), 512)], axis=0)
+    first_part, last_part = slice(0, 256), slice(256, 512)
+    upper = lower = jnp.zeros((256, B), f32)
+    for start, size in LANES:
+        lanes = slice(start, start + size)
+        r = mm3((inv_hi[:, :256], inv_lo[:, :256]), split(w_sum[first_part, lanes]), NN)
+        upper = keep(first_part, lanes, r[:256], upper)
+        for i in range(4):
+            w_recv0[i, :, lanes] = r[256 + 64 * i : 320 + 64 * i]
+    finish(w5[2] + w5[3])
+    for start, size in LANES:
+        lanes = slice(start, start + size)
+        r = mm3((inv_hi[256:, 256:], inv_lo[256:, 256:]), split(w_sum[last_part, lanes]), NN)
+        r = r + jnp.concatenate([w_recv0[i, :, lanes] for i in range(4)], axis=0)
+        lower = keep(last_part, lanes, r, lower)
+    squares = jnp.concatenate([upper, lower], axis=0)
     saves = []
 
     def save(src, dst):
@@ -472,9 +521,9 @@
             pltpu.VMEM((R, C), bf16),
             pltpu.VMEM((R, C), bf16),
             pltpu.VMEM((4, R, B), f32),
-            pltpu.VMEM((4, 3, 256, B), f32),
-            pltpu.VMEM((4, 256, B), f32),
-            pltpu.VMEM((4, 3, 64, B), f32),
+            pltpu.VMEM((4, 2, 3, 128, B), f32),
+            pltpu.VMEM((4, 2, 128, B), f32),
+            pltpu.VMEM((4, 2, 3, 32, B), f32),
             pltpu.VMEM((4, R, B), f32),
             pltpu.VMEM((RANK, R), bf16),
             pltpu.VMEM((RANK, R), bf16),
@@ -484,9 +533,9 @@
             pltpu.VMEM((1280, B), f32),
             pltpu.VMEM((RANK, RANK), f32),
             pltpu.VMEM((RANK, RANK), f32),
-            pltpu.VMEM((2, B, C), f32),
-            pltpu.VMEM((2, 64, C), f32),
-            pltpu.VMEM((2, 32, C), f32),
+            pltpu.VMEM((4, 64, C), f32),
+            pltpu.VMEM((4, 32, C), f32),
+            pltpu.VMEM((4, 16, C), f32),
             pltpu.VMEM((R, RANK), f32),
             pltpu.VMEM((8, RANK), f32),
             pltpu.VMEM((15, 8, RANK), f32),

time: 126 us -> 114 us (0.905)
  Pallas kernels: 122 us -> 111 us
    pallas_call x1, Pallas kernels: 111 us -> 100 us  [sums(): pl.pallas_call(sum_kernel, out_shape=[jax.ShapeDtypeStruct((R, RANK), f32...]
where the time goes in v5:
time: 114 us; the launch traced here: 113 us
  Pallas kernels  111 us (97%)
  local copies, waits for them, and re-layouts  1.45 us (1%)
    pallas_call x1, Pallas kernels, sums(): pl.pallas_call(sum_kernel, out_shape=[jax.ShapeDtypeStruct((R, RANK), f32...  100 us
    pallas_call x1, Pallas kernels, outputs(): pl.pallas_call(output_kernel, grid=(STEPS,), out_shape=[jax.ShapeDtypeStr...  10.9 us

profile of v5, /device:TPU:0, one launch (start us, length us, event | category | flops | bytes accessed | tf_op | source)
XLA Modules:
  0.0 113.4 jit_solution(714159918790337864)
XLA Ops:
  0.6 0.0 copy-start.2
  0.6 1.4 %copy-done.2 = bf16[1664,512]{1,0:T(8,128)(2,1)S(1)} copy-done((bf16[1664,512]{1,0:T(8,128)(2,1)S(1)}, bf16[1664,512]{1,0:T(8,128)(2,1)}, u32[]{:S(2)}) %copy-start.2) | copy-done | bytes 1703960
  2.1 0.0 copy-start
  2.1 0.0 copy-start.1
  2.1 100.4 %sums.1 = (f32[1024,512]{1,0:T(8,128)S(1)}, bf16[512,1664]{1,0:T(8,128)(2,1)S(1)}, bf16[512,1664]{1,0:T(8,128)(2,1)S(1)}, f32[8,512]{1,0:T(8,128)S(1)}) custom-call(f32[1024,1664]{1,0:T(8,128)} %mom.1, bf16[1024,1664]{1,0:T(8,128)(2,1)} %grad.1, bf16[1664,512]{1,0:T(8,128)(2,1)S(1)} %copy-done.2), custom_call_target="tpu_custom_call" | custom-call | tf_op jit(solution)/shard_map/sums/pallas_call | solution.py:507
  102.5 0.0 copy-done
  102.5 0.0 copy-done.1
  102.5 10.9 %outputs.1 = (f32[1024,1664]{1,0:T(8,128)}, bf16[1664,512]{1,0:T(8,128)(2,1)}, bf16[1024,1664]{1,0:T(8,128)(2,1)}) custom-call(f32[1024,1664]{1,0:T(8,128)S(1)} %copy-done, bf16[1024,1664]{1,0:T(8,128)(2,1)S(1)} %copy-done.1, f32[1024,512]{1,0:T(8,128)S(1)} %get-tuple-element.7.orth_ref, bf16[512,1664]{1,0:T(8,128)(2,1)S(1)} %get-tuple-element.8.r_hi, ...), custom_call_target="tpu_custom_call" | custom-call | tf_op jit(solution)/shard_map/outputs/pallas_call | solution.py:583
Async XLA Ops:
  0.6 1.5 %copy-start.2 = (bf16[1664,512]{1,0:T(8,128)(2,1)S(1)}, bf16[1664,512]{1,0:T(8,128)(2,1)}, u32[]{:S(2)}) copy-start(bf16[1664,512]{1,0:T(8,128)(2,1)} %q_hbm.1) | copy-start | bytes 5111812
  2.1 100.4 %copy-start = (f32[1024,1664]{1,0:T(8,128)S(1)}, f32[1024,1664]{1,0:T(8,128)}, u32[]{:S(2)}) copy-start(f32[1024,1664]{1,0:T(8,128)} %mom.1) | copy-start | bytes 20447236
  2.1 100.4 %copy-start.1 = (bf16[1024,1664]{1,0:T(8,128)(2,1)S(1)}, bf16[1024,1664]{1,0:T(8,128)(2,1)}, u32[]{:S(2)}) copy-start(bf16[1024,1664]{1,0:T(8,128)(2,1)} %grad.1) | copy-start | bytes 10223620

commit v6 on v5

--- a/solution.py
+++ b/solution.py
@@ -96,28 +96,37 @@
 
 
 def factor_step(k, diagonal, gram, inv):
-    o, p, n = B * k, B * (k + 1), B * (k + 2)
+    o, p, n, end = B * k, B * (k + 1), B * (k + 2), B * 3
     x = inverse_factor(diagonal)
     inv[o:p, o:p] = x
-    if k < 3:
+    if k < 2:
         near = mm6(gram[p:n, o:p], x, NT)
         diagonal = gram[p:n, p:n] - mm6(near, near, NT)
     if k > 0:
         inv[o:p, 0:o] = mm6(x, inv[o:p, 0:o], NN)
-    if k < 3:
+    if k < 2:
         low = near
-        if k < 2:
-            far = mm6(gram[n:, o:p], x, NT)
-            gram[n:, p:n] = gram[n:, p:n] - mm6(far, near, NT)
-            gram[n:, n:] = gram[n:, n:] - mm6(far, far, NT)
+        if k == 0:
+            far = mm6(gram[n:end, o:p], x, NT)
+            gram[n:end, p:n] = gram[n:end, p:n] - mm6(far, near, NT)
+            gram[n:end, n:end] = gram[n:end, n:end] - mm6(far, far, NT)
             low = jnp.concatenate([near, far], axis=0)
-        inv[p:, 0:p] = inv[p:, 0:p] - mm6(low, inv[o:p, 0:p], NN)
+        inv[p:end, 0:p] = inv[p:end, 0:p] - mm6(low, inv[o:p, 0:p], NN)
     return diagonal
 
 
-PACKED = [(0, 0), (1, 0), (1, 1), (2, 0), (2, 1), (2, 2), (3, 0), (3, 1), (3, 2), (3, 3)]
+def last_step(gram, inv):
+    end = B * 3
+    others = inv[0:end, 0:end]
+    low = mm6(gram[end:, 0:end], others, NT)
+    x = inverse_factor(gram[end:, end:] - mm6(low, low, NT))
+    inv[end:, end:] = x
+    inv[end:, 0:end] = -mm6(x, mm6(low, others, NN), NN)
+
+
+GRAM_PARTS = ((0, 768, 0, 0), (768, 512, 384, 96))
 LANES = [(256 * j, min(256, C - 256 * j)) for j in range(7)]
-N_MSG = 159
+N_MSG = 167
 
 
 def sum_kernel(
@@ -253,13 +262,42 @@
             rows = slice(256 * i, 256 * i + 256)
             pt_hi[B * s : B * s + B, rows], pt_lo[B * s : B * s + B, rows] = split(p_buf[s, rows, :].T)
 
-    def gram_block(s, t):
-        a, b = slice(256 * s, 256 * s + 256), slice(256 * t, 256 * t + 256)
+    def gram_row(i):
+        a, b = slice(B * i, B * i + B), slice(0, B * i + B)
         value = mm(pt_lo[a, :], pt_lo[b, :], NT) + mm3((pt_hi[a, :], pt_lo[a, :]), (pt_hi[b, :], pt_lo[b, :]), NT)
-        for n, (i, j) in enumerate(PACKED):
-            if i // 2 == s and j // 2 == t:
-                r, c = B * (i % 2), B * (j % 2)
-                packed[B * n : B * n + B, :] = value[r : r + B, c : c + B]
+        for j in range(i + 1):
+            start = B * (i * (i + 1) // 2 + j)
+            packed[start : start + B, :] = value[:, B * j : B * j + B]
+
+    def g_half(part, which):
+        base, size, _, _ = GRAM_PARTS[part]
+        return pl.ds(pl.multiple_of(base + which * (size // 2), 32), size // 2)
+
+    def g_slab(part, i):
+        base, size, _, _ = GRAM_PARTS[part]
+        return pl.ds(pl.multiple_of(base + core * (size // 2) + i * (size // 8), 32), size // 8)
+
+    def g_cores(part):
+        _, size, at, _ = GRAM_PARTS[part]
+        return [send(packed.at[g_half(part, 1 - core)], g_recv0.at[at : at + size // 2], other_core)]
+
+    def g_scatter(part):
+        _, size, at, to = GRAM_PARTS[part]
+        ours = g_half(part, core)
+        packed[ours, :] = packed[ours, :] + g_recv0[at : at + size // 2, :]
+        return [
+            send(packed.at[g_slab(part, (x + d) % 4)], g_recv1.at[d - 1, to : to + size // 8], at_x(d)) for d in (2, 1, 3)
+        ]
+
+    def g_gather(part):
+        _, size, _, to = GRAM_PARTS[part]
+        mine, here = g_slab(part, x), slice(to, to + size // 8)
+        g_sum[mine, :] = (packed[mine, :] + g_recv1[0, here, :]) + (g_recv1[1, here, :] + g_recv1[2, here, :])
+        return [send(g_sum.at[mine], g_sum.at[mine], at_x(d)) for d in (2, 1, 3)]
+
+    def g_back(part):
+        ours = g_half(part, core)
+        return [send(g_sum.at[ours], g_sum.at[ours], other_core)]
 
     def product_w(s):
         rows = slice(B * s, B * s + B)
@@ -386,69 +424,79 @@
         finish(w4[s])
         w5[s] = w_back(s)
 
+    on = lax.broadcasted_iota(jnp.int32, (B, B), 0) == lax.broadcasted_iota(jnp.int32, (B, B), 1)
+    across = []
+
+    def scaled_row(i):
+        start = B * (i * (i + 1) // 2)
+        square = jnp.where(on, g_sum[start + B * i : start + B * i + B, :], 0.0)
+        down = lax.rsqrt(jnp.sum(square, axis=1, keepdims=True))
+        across.append(lax.rsqrt(jnp.sum(square, axis=0, keepdims=True)))
+        for j in range(i + 1):
+            value = g_sum[start + B * j : start + B * j + B, :]
+            gram[B * i : B * i + B, B * j : B * j + B] = value * down * across[j]
+
     finish(p4[0])
     transpose_p(0)
     start_w(0)
+    gram_row(0)
     finish(p3[3])
     p4[3] = gather_first(3)
     finish(p4[1])
     transpose_p(1)
     start_w(1)
     scatter_far(0)
+    gram_row(1)
     scatter_far(1)
-    gram_block(0, 0)
     finish(p4[2])
     transpose_p(2)
+    gram_row(2)
+    a0 = g_cores(0)
+    inv[...] = jnp.zeros((RANK, RANK), f32)
+    finish(a0)
+    a1 = g_scatter(0)
     finish(p4[3])
     transpose_p(3)
-    gram_block(1, 0)
-    gram_block(1, 1)
-    g_ours, g_theirs = block(640 * core, 640), block(640 * (1 - core), 640)
-    g0 = [send(packed.at[g_theirs], g_recv0, other_core)]
+    gram_row(3)
+    b0 = g_cores(1)
     scatter_near(0)
-    finish(g0)
-    packed[g_ours, :] = packed[g_ours, :] + g_recv0[...]
-
-    def g_slab(i):
-        return block(640 * core + 160 * i, 160)
-
-    g1 = [send(packed.at[g_slab((x + d) % 4)], g_recv1.at[d - 1], at_x(d)) for d in (2, 1, 3)]
+    finish(a1)
+    a2 = g_gather(0)
+    finish(b0)
+    b1 = g_scatter(1)
+    start_w(2)
     scatter_near(1)
-    start_w(2)
+    finish(a2)
+    a3 = g_back(0)
+    finish(b1)
+    b2 = g_gather(1)
+    gather_near(0)
     start_w(3)
-    inv[...] = jnp.zeros((RANK, RANK), f32)
-    finish(g1)
-    g_mine = g_slab(x)
-    g_sum[g_mine, :] = (packed[g_mine, :] + g_recv1[0]) + (g_recv1[1] + g_recv1[2])
-    g2 = [send(g_sum.at[g_mine], g_sum.at[g_mine], at_x(d)) for d in (2, 1, 3)]
-    gather_near(0)
+    finish(a3)
+    for i in range(3):
+        scaled_row(i)
     gather_near(1)
-    finish(g2)
-    g3 = [send(g_sum.at[g_ours], g_sum.at[g_ours], other_core)]
     scatter_far(2)
     scatter_far(3)
-    finish(g3)
-    on = lax.broadcasted_iota(jnp.int32, (B, B), 0) == lax.broadcasted_iota(jnp.int32, (B, B), 1)
-    diagonals = [jnp.where(on, g_sum[B * n : B * n + B, :], 0.0) for n in (0, 2, 5, 9)]
-    down = [lax.rsqrt(jnp.sum(t, axis=1, keepdims=True)) for t in diagonals]
-    across = [lax.rsqrt(jnp.sum(t, axis=0, keepdims=True)) for t in diagonals]
-    for n, (i, j) in enumerate(PACKED):
-        gram[B * i : B * i + B, B * j : B * j + B] = g_sum[B * n : B * n + B, :] * down[i] * across[j]
 
     diagonal = factor_step(0, gram[0:B, 0:B], gram, inv)
+    finish(b2)
+    b3 = g_back(1)
     scatter_near(2)
     scatter_near(3)
     gather_far(0)
     gather_far(1)
     diagonal = factor_step(1, diagonal, gram, inv)
+    finish(b3)
+    scaled_row(3)
     gather_near(2)
     gather_near(3)
-    diagonal = factor_step(2, diagonal, gram, inv)
+    factor_step(2, diagonal, gram, inv)
     gather_far(2)
     gather_far(3)
     gather_cores(0)
     gather_cores(1)
-    factor_step(3, diagonal, gram, inv)
+    last_step(gram, inv)
     gather_cores(2)
     gather_cores(3)
     inv_hi, inv_lo = split(inv[...] * jnp.concatenate(across, axis=1))

time: 114 us -> 112 us (0.982)
  Pallas kernels: 111 us -> 109 us
    pallas_call x1, Pallas kernels: 100 us -> 98.4 us  [sums(): pl.pallas_call(sum_kernel, out_shape=[jax.ShapeDtypeStruct((R, RANK), f32...]
where the time goes in v6:
time: 112 us; the launch traced here: 111 us
  Pallas kernels  109 us (97%)
  local copies, waits for them, and re-layouts  1.45 us (1%)
    pallas_call x1, Pallas kernels, sums(): pl.pallas_call(sum_kernel, out_shape=[jax.ShapeDtypeStruct((R, RANK), f32...  98.4 us
    pallas_call x1, Pallas kernels, outputs(): pl.pallas_call(output_kernel, grid=(STEPS,), out_shape=[jax.ShapeDtypeStr...  10.8 us

profile of v6, /device:TPU:0, one launch (start us, length us, event | category | flops | bytes accessed | tf_op | source)
XLA Modules:
  0.0 111.4 jit_solution(4372045993753470719)
XLA Ops:
  0.6 0.0 copy-start.2
  0.6 1.4 %copy-done.2 = bf16[1664,512]{1,0:T(8,128)(2,1)S(1)} copy-done((bf16[1664,512]{1,0:T(8,128)(2,1)S(1)}, bf16[1664,512]{1,0:T(8,128)(2,1)}, u32[]{:S(2)}) %copy-start.2) | copy-done | bytes 1703960
  2.1 0.0 copy-start
  2.1 0.0 copy-start.1
  2.1 98.4 %sums.1 = (f32[1024,512]{1,0:T(8,128)S(1)}, bf16[512,1664]{1,0:T(8,128)(2,1)S(1)}, bf16[512,1664]{1,0:T(8,128)(2,1)S(1)}, f32[8,512]{1,0:T(8,128)S(1)}) custom-call(f32[1024,1664]{1,0:T(8,128)} %mom.1, bf16[1024,1664]{1,0:T(8,128)(2,1)} %grad.1, bf16[1664,512]{1,0:T(8,128)(2,1)S(1)} %copy-done.2), custom_call_target="tpu_custom_call" | custom-call | tf_op jit(solution)/shard_map/sums/pallas_call | solution.py:555
  100.5 0.0 copy-done
  100.5 0.0 copy-done.1
  100.6 10.8 %outputs.1 = (f32[1024,1664]{1,0:T(8,128)}, bf16[1664,512]{1,0:T(8,128)(2,1)}, bf16[1024,1664]{1,0:T(8,128)(2,1)}) custom-call(f32[1024,1664]{1,0:T(8,128)S(1)} %copy-done, bf16[1024,1664]{1,0:T(8,128)(2,1)S(1)} %copy-done.1, f32[1024,512]{1,0:T(8,128)S(1)} %get-tuple-element.7.orth_ref, bf16[512,1664]{1,0:T(8,128)(2,1)S(1)} %get-tuple-element.8.r_hi, ...), custom_call_target="tpu_custom_call" | custom-call | tf_op jit(solution)/shard_map/outputs/pallas_call | solution.py:631
Async XLA Ops:
  0.6 1.5 %copy-start.2 = (bf16[1664,512]{1,0:T(8,128)(2,1)S(1)}, bf16[1664,512]{1,0:T(8,128)(2,1)}, u32[]{:S(2)}) copy-start(bf16[1664,512]{1,0:T(8,128)(2,1)} %q_hbm.1) | copy-start | bytes 5111812
  2.1 98.4 %copy-start = (f32[1024,1664]{1,0:T(8,128)S(1)}, f32[1024,1664]{1,0:T(8,128)}, u32[]{:S(2)}) copy-start(f32[1024,1664]{1,0:T(8,128)} %mom.1) | copy-start | bytes 20447236
  2.1 98.5 %copy-start.1 = (bf16[1024,1664]{1,0:T(8,128)(2,1)S(1)}, bf16[1024,1664]{1,0:T(8,128)(2,1)}, u32[]{:S(2)}) copy-start(bf16[1024,1664]{1,0:T(8,128)(2,1)} %grad.1) | copy-start | bytes 10223620

commit v7 on v6

--- a/solution.py
+++ b/solution.py
@@ -455,6 +455,7 @@
     inv[...] = jnp.zeros((RANK, RANK), f32)
     finish(a0)
     a1 = g_scatter(0)
+    start_w(2)
     finish(p4[3])
     transpose_p(3)
     gram_row(3)
@@ -464,7 +465,6 @@
     a2 = g_gather(0)
     finish(b0)
     b1 = g_scatter(1)
-    start_w(2)
     scatter_near(1)
     finish(a2)
     a3 = g_back(0)

time: 112 us -> 113 us (level)
  Pallas kernels: 109 us -> 111 us
    pallas_call x1, Pallas kernels: 98.4 us -> 99.7 us  [sums(): pl.pallas_call(sum_kernel, out_shape=[jax.ShapeDtypeStruct((R, RANK), f32...]
where the time goes in v7:
time: 113 us
  Pallas kernels  111 us (98%)
  local copies, waits for them, and re-layouts  1.45 us (1%)
    pallas_call x1, Pallas kernels, sums(): pl.pallas_call(sum_kernel, out_shape=[jax.ShapeDtypeStruct((R, RANK), f32...  99.7 us
    pallas_call x1, Pallas kernels, outputs(): pl.pallas_call(output_kernel, grid=(STEPS,), out_shape=[jax.ShapeDtypeStr...  10.9 us

profile of v7, /device:TPU:0, one launch (start us, length us, event | category | flops | bytes accessed | tf_op | source)
XLA Modules:
  0.0 112.7 jit_solution(9089622008535385780)
XLA Ops:
  0.6 0.0 copy-start.2
  0.6 1.4 %copy-done.2 = bf16[1664,512]{1,0:T(8,128)(2,1)S(1)} copy-done((bf16[1664,512]{1,0:T(8,128)(2,1)S(1)}, bf16[1664,512]{1,0:T(8,128)(2,1)}, u32[]{:S(2)}) %copy-start.2) | copy-done | bytes 1703960
  2.1 0.0 copy-start
  2.1 0.0 copy-start.1
  2.1 99.7 %sums.1 = (f32[1024,512]{1,0:T(8,128)S(1)}, bf16[512,1664]{1,0:T(8,128)(2,1)S(1)}, bf16[512,1664]{1,0:T(8,128)(2,1)S(1)}, f32[8,512]{1,0:T(8,128)S(1)}) custom-call(f32[1024,1664]{1,0:T(8,128)} %mom.1, bf16[1024,1664]{1,0:T(8,128)(2,1)} %grad.1, bf16[1664,512]{1,0:T(8,128)(2,1)S(1)} %copy-done.2), custom_call_target="tpu_custom_call" | custom-call | tf_op jit(solution)/shard_map/sums/pallas_call | solution.py:555
  101.8 0.0 copy-done
  101.8 0.0 copy-done.1
  101.8 10.9 %outputs.1 = (f32[1024,1664]{1,0:T(8,128)}, bf16[1664,512]{1,0:T(8,128)(2,1)}, bf16[1024,1664]{1,0:T(8,128)(2,1)}) custom-call(f32[1024,1664]{1,0:T(8,128)S(1)} %copy-done, bf16[1024,1664]{1,0:T(8,128)(2,1)S(1)} %copy-done.1, f32[1024,512]{1,0:T(8,128)S(1)} %get-tuple-element.7.orth_ref, bf16[512,1664]{1,0:T(8,128)(2,1)S(1)} %get-tuple-element.8.r_hi, ...), custom_call_target="tpu_custom_call" | custom-call | tf_op jit(solution)/shard_map/outputs/pallas_call | solution.py:631
Async XLA Ops:
  0.6 1.5 %copy-start.2 = (bf16[1664,512]{1,0:T(8,128)(2,1)S(1)}, bf16[1664,512]{1,0:T(8,128)(2,1)}, u32[]{:S(2)}) copy-start(bf16[1664,512]{1,0:T(8,128)(2,1)} %q_hbm.1) | copy-start | bytes 5111812
  2.1 99.7 %copy-start = (f32[1024,1664]{1,0:T(8,128)S(1)}, f32[1024,1664]{1,0:T(8,128)}, u32[]{:S(2)}) copy-start(f32[1024,1664]{1,0:T(8,128)} %mom.1) | copy-start | bytes 20447236
  2.1 99.7 %copy-start.1 = (bf16[1024,1664]{1,0:T(8,128)(2,1)S(1)}, bf16[1024,1664]{1,0:T(8,128)(2,1)}, u32[]{:S(2)}) copy-start(bf16[1024,1664]{1,0:T(8,128)(2,1)} %grad.1) | copy-start | bytes 10223620
